TPU v7x, 32 devices: a whole 2x2x4 slice. The times are simulated.
32 devices in a mesh: tbit: 4 (over y, x), box: 8 (over z, core).
Axes of the slice: x: 2, y: 2, z: 4, core: 2. Of those that a mesh axis runs over, the one named last changes fastest.
Arguments:
- coeffs: float32 [64, 16, 4, 64, 256], P(None, 'box', 'tbit'), may hold values from -6 to 6
- skeleton_first: int32 [64, 16, 4, 64], P(None, 'box'), may hold values from 0 to 16383, as said below
- skeleton_second: int32 [64, 16, 4, 64], P(None, 'box'), may hold values from 0 to 32767, as said below
- skeleton_third: int32 [64, 16, 4, 64], P(None, 'box'), may hold values from 0 to 65535, as said below
- checks_first: int32 [128, 64], replicated, may hold values from 0 to 8191, as said below
- checks_second: int32 [256, 64], replicated, may hold values from 0 to 4095, as said below
- checks_third: int32 [512, 64], replicated, may hold values from 0 to 2047, as said below
- ranks_first: int32 [64, 16, 4], P(None, 'box', 'tbit'), may hold values from 32 to 64
- ranks_second: int32 [64, 16, 4], P(None, 'box', 'tbit'), may hold values from 32 to 64
- ranks_third: int32 [64, 4, 2, 8], replicated, may hold values from 32 to 64
- interpolants: float32 [3, 64, 64], replicated, may hold values from -0.09375 to 0.09375
- owners: int32 [4, 64], replicated, may hold values from 0 to 7, as said below
Outputs:
- switched: float32 [4, 8, 2, 16, 8, 64, 256], P('tbit', 'box')
Inputs may be any that keep to these rules, and one draw needn't show every extreme that they name: `skeleton_first`: entry r lies in the r-th of 64 equal parts of its source box of 16384 points. `skeleton_second`: entry r lies in the r-th of 64 equal parts of its source box of 32768 points. `skeleton_third`: entry r lies in the r-th of 64 equal parts of its source box of 65536 points. `checks_first`: entry r lies in the r-th of 64 equal parts of its target box. `checks_second`: entry r lies in the r-th of 64 equal parts of its target box. `checks_third`: entry r lies in the r-th of 64 equal parts of its target box. `owners`: in each row no box index is named more than 16 times, and some index exactly 16 times.
All inputs are finite; a program needn't handle non-finite values.
Results may differ from a plain program's by a relative error of at most 0.0003.
Values sent between devices are 32-bit elements; how exact they have to be, the bound alone decides.
No kernel may reach another device: no remote copies, remote signals or barrier semaphores. Data moves between devices by JAX's collectives and lax.ppermute only.
A program may use at most 128 MiB of HBM per device.

v0:
```python
import math

import jax
import jax.numpy as jnp
from jax import lax
from jax.sharding import PartitionSpec as P

NPTS = 1048576


two_pi = 2.0 * math.pi
highest = lax.Precision.HIGHEST


def swapped(value, axis, bit):
    mask = 2**bit
    pairs = [(source, source ^ mask) for source in range(lax.axis_size(axis))]
    return lax.ppermute(value, axis, pairs)


def kernel_block(targets, sources):
    target_rows = targets[..., :, None]
    source_cols = sources[..., None, :]
    upper_part = target_rows // 1024
    lower_part = target_rows % 1024
    phases = (upper_part * source_cols % 1024 * 1024 + lower_part * source_cols) % NPTS
    return jnp.cos(phases.astype(jnp.float32) * (two_pi / NPTS))


def slot_table(owner_row, box_count, capacity):
    parent_count = owner_row.shape[0]
    onehot = (owner_row[:, None] == jnp.arange(box_count, dtype=jnp.int32)[None, :]).astype(
        jnp.int32
    )
    earlier = jnp.cumsum(onehot, axis=0, dtype=jnp.int32) - onehot
    slot_of = jnp.sum(earlier * onehot, axis=1, dtype=jnp.int32)
    matches = (onehot.T[:, None, :] == 1) & (
        slot_of[None, None, :] == jnp.arange(capacity, dtype=jnp.int32)[None, :, None]
    )
    slot_parent = jnp.sum(
        jnp.where(matches, jnp.arange(parent_count, dtype=jnp.int32)[None, None, :], 0), axis=2
    )
    slot_used = jnp.any(matches, axis=2)
    return (slot_parent, slot_used)


def pick_slot(values, position):
    return lax.dynamic_index_in_dim(values, position, 2, keepdims=False)


def partner_level(
    mine_coeffs, mine_points, other_points, targets_both, matrix, rank_rows, swap_bit, mine_child
):
    rank_width = matrix.shape[0]
    parent_count = mine_coeffs.shape[0]
    arrived = swapped(mine_coeffs, "tbit", swap_bit)
    my_targets = lax.dynamic_index_in_dim(
        targets_both.reshape(parent_count, 2, rank_width), mine_child, 1, keepdims=False
    )
    kernels = kernel_block(
        my_targets[:, None, :], jnp.concatenate([mine_points, other_points], axis=2)
    )
    images = jnp.einsum(
        "ahcs,ahsn->ahcn",
        kernels,
        jnp.concatenate([mine_coeffs, arrived], axis=2),
        precision=highest,
    )
    merged = jnp.einsum("ij,ahjn->ahin", matrix, images, precision=highest)
    live_rows = jnp.arange(rank_width, dtype=jnp.int32)[None, None, :] < rank_rows[:, :, None]
    return jnp.where(live_rows[..., None], merged, 0.0)


def per_device(
    coeffs,
    skeleton_first,
    skeleton_second,
    skeleton_third,
    checks_first,
    checks_second,
    checks_third,
    ranks_first,
    ranks_second,
    ranks_third,
    interpolants,
    owners,
):
    tbit_index = lax.axis_index("tbit")
    box_index = lax.axis_index("box")
    box_count = lax.axis_size("box")
    parent_count = coeffs.shape[0]
    rank_width = coeffs.shape[3]
    capacity = 2 * parent_count // box_count
    group_count = 2 * box_count
    local_boxes = 2 * box_index + jnp.arange(2, dtype=jnp.int32)[None, :, None, None]
    four_slots = jnp.arange(4, dtype=jnp.int32)[None, None, :, None]
    points_first = (4 * local_boxes + 2 * (four_slots % 2) + four_slots // 2) * (
        NPTS // (4 * group_count)
    ) + skeleton_first
    points_second = (2 * local_boxes + four_slots % 2) * (
        NPTS // (2 * group_count)
    ) + skeleton_second
    points_third = local_boxes * (NPTS // group_count) + skeleton_third
    targets_first = (
        jnp.arange(2 * parent_count, dtype=jnp.int32)[:, None] * (NPTS // (2 * parent_count))
        + checks_first
    )
    targets_second = (
        jnp.arange(4 * parent_count, dtype=jnp.int32)[:, None] * (NPTS // (4 * parent_count))
        + checks_second
    )
    targets_third = (
        jnp.arange(8 * parent_count, dtype=jnp.int32)[:, None] * (NPTS // (8 * parent_count))
        + checks_third
    )
    partner_high = jnp.bitwise_xor(tbit_index, 2)
    partner_low = jnp.bitwise_xor(tbit_index, 1)
    merged_one = partner_level(
        coeffs[:, :, 0],
        pick_slot(points_first, tbit_index),
        pick_slot(points_first, partner_high),
        targets_first.reshape(parent_count, 2 * rank_width),
        interpolants[0],
        ranks_first[:, :, 0],
        1,
        tbit_index // 2,
    )
    second_targets = lax.dynamic_index_in_dim(
        targets_second.reshape(parent_count, 2, 2 * rank_width), tbit_index // 2, 1, keepdims=False
    )
    merged_two = partner_level(
        merged_one,
        pick_slot(points_second, tbit_index),
        pick_slot(points_second, partner_low),
        second_targets,
        interpolants[1],
        ranks_second[:, :, 0],
        0,
        tbit_index % 2,
    )
    third_points = pick_slot(points_third, tbit_index)
    targets_mine = lax.dynamic_index_in_dim(
        targets_third.reshape(parent_count, 4, 2 * rank_width), tbit_index, 1, keepdims=False
    )
    slot_parent, slot_used = slot_table(
        lax.dynamic_index_in_dim(owners, tbit_index, 0, keepdims=False), box_count, capacity
    )
    rank_mine = lax.dynamic_index_in_dim(ranks_third, tbit_index, 1, keepdims=False)
    parent_rows = slot_parent.T
    used_rows = slot_used.T
    kernels = kernel_block(targets_mine, third_points.reshape(parent_count, 2 * rank_width))
    images = jnp.einsum(
        "acs,asn->acn",
        kernels,
        merged_two.reshape(parent_count, 2 * rank_width, merged_two.shape[-1]),
        precision=highest,
    )
    images = images.reshape(parent_count, 2, rank_width, images.shape[-1])
    merged = jnp.einsum("ij,atjn->tain", interpolants[2], images, precision=highest)
    own_ranks = lax.dynamic_index_in_dim(rank_mine, box_index, 2, keepdims=False)
    live_rows = jnp.arange(rank_width, dtype=jnp.int32)[None, None, :] < own_ranks.T[:, :, None]
    merged = jnp.where(live_rows[..., None], merged, 0.0)
    outgoing = jnp.take(merged, parent_rows, axis=1)
    outgoing = jnp.where(used_rows[None, :, :, None, None], outgoing, 0.0)
    switched = lax.all_to_all(outgoing, "box", split_axis=2, concat_axis=2, tiled=True)
    return switched[None, None]


def solution(mesh):
    return jax.shard_map(
        per_device,
        mesh=mesh,
        in_specs=(
            P(None, "box", "tbit", None, None),
            P(None, "box", None, None),
            P(None, "box", None, None),
            P(None, "box", None, None),
            P(),
            P(),
            P(),
            P(None, "box", "tbit"),
            P(None, "box", "tbit"),
            P(),
            P(),
            P(),
        ),
        out_specs=P("tbit", "box", None, None, None, None, None),
        check_vma=False,
    )
```

profile of v0, /device:TPU:0, one launch (start us, length us, event | category | flops | bytes accessed | tf_op | source)
XLA Modules:
  0.0 885.4 jit_solution(3372632769682777200)
XLA Ops:
  0.0 3.0 collective-permute-start
  3.0 0.8 copy.56
  3.7 0.8 copy.57
  4.9 1.1 broadcast_add_fusion
  6.0 0.1 pad_add_fusion.1
  6.4 177.4 %collective-permute-done = f32[64,2,64,256]{3,2,1,0:T(8,128)} collective-permute-done((f32[64,2,64,256]{3,2,1,0:T(8,128)}, f32[64,2,64,256]{3,2,1,0:T(8,128)}, u32[]{:S(2)}, u32[]{:S(2)}) %collective-permute-start) | collective-permute-done | bytes 8388640 | tf_op jit(solution)/shard_map/ppermute | solution.py:18
  183.7 31.2 %fusion = f32[64,2,64,256]{3,2,1,0:T(8,128)S(1)} fusion(f32[64,2,64,256]{3,2,1,0:T(8,128)} %collective-permute-done, f32[64,2,64,256]{3,2,1,0:T(8,128)} %bitcast.75, s32[64,64]{1,0:T(8,128)S(1)} %get-tuple-element.14, s32[64,2,128]{2,1,0:T(2,128)S(1)} %pad_add_fusion.1, s32[64,64]{1,0:T(8,128)S(1)} %get-tuple-element.13), kind=kOutput, calls=%fused_computation.1 | convolution fusion | flops 3254779904 | bytes 25264128 | tf_op jit(solution)/shard_map/ahcs,ahsn->ahcn/dot_general | solution.py:63
  215.0 9.8 %select_bitcast_fusion = f32[64,2,64,256]{3,2,1,0:T(8,128)} fusion(pred[64,2,64]{2,1,0:T(4,128)(4,1)S(1)} %iota_compare_fusion, f32[64,2,64,256]{3,2,1,0:T(8,128)S(1)} %fusion, f32[3,64,64]{2,1,0:T(8,128)S(1)} %copy-done.4), kind=kOutput, calls=%fused_computation.13 | convolution fusion | flops 1612709888 | bytes 16842752 | tf_op jit(solution)/shard_map/ij,ahjn->ahin/dot_general | solution.py:69
  224.7 1.8 collective-permute-start.1
  226.6 0.7 fusion.98
  227.5 0.2 select_reduce_fusion
  227.7 0.2 fusion.80
  228.2 1.2 fusion.81
  230.4 0.2 and_reduce_fusion
  230.9 0.1 pad_add_fusion
  231.4 175.3 %collective-permute-done.1 = f32[64,2,64,256]{3,2,1,0:T(8,128)} collective-permute-done((f32[64,2,64,256]{3,2,1,0:T(8,128)}, f32[64,2,64,256]{3,2,1,0:T(8,128)}, u32[]{:S(2)}, u32[]{:S(2)}) %collective-permute-start.1) | collective-permute-done | bytes 8388640 | tf_op jit(solution)/shard_map/ppermute | solution.py:18
  406.7 31.3 %fusion.4 = f32[64,2,64,256]{3,2,1,0:T(8,128)S(1)} fusion(f32[64,2,64,256]{3,2,1,0:T(8,128)} %collective-permute-done.1, f32[64,2,64,256]{3,2,1,0:T(8,128)} %select_bitcast_fusion, s32[64,64]{1,0:T(8,128)S(1)} %get-tuple-element.12, s32[64,2,128]{2,1,0:T(2,128)S(1)} %pad_add_fusion, s32[64,64]{1,0:T(8,128)S(1)} %get-tuple-element.11), kind=kOutput, calls=%fused_computation.5 | convolution fusion | flops 3254779904 | bytes 25264128 | tf_op jit(solution)/shard_map/ahcs,ahsn->ahcn/dot_general | solution.py:63
  438.0 8.4 broadcast_select_fusion
  446.4 32.5 %fusion.16 = f32[64,128,256]{2,1,0:T(8,128)S(1)} fusion(f32[64,128,256]{2,1,0:T(8,128)S(1)} %bitcast.60, s32[64,128]{1,0:T(8,128)S(1)} %get-tuple-element.10, s32[64,128]{1,0:T(8,128)S(1)} %mul.189, s32[64,128]{1,0:T(8,128)S(1)} %get-tuple-element.9), kind=kOutput, calls=%fused_computation.44 | convolution fusion | flops 3250585600 | bytes 16875520 | tf_op jit(solution)/shard_map/acs,asn->acn/dot_general | solution.py:152
  478.9 9.8 %bitcast_select_fusion = f32[2,64,64,256]{3,2,0,1:T(8,128)} fusion(pred[2,64,64]{2,0,1:T(4,128)(4,1)S(1)} %iota_compare_fusion.2, f32[64,2,64,256]{3,2,1,0:T(8,128)S(1)} %bitcast.61, f32[3,64,64]{2,1,0:T(8,128)S(1)} %copy-done.4), kind=kOutput, calls=%fused_computation.12 | convolution fusion | flops 1612709888 | bytes 16842752 | tf_op jit(solution)/shard_map/ij,atjn->tain/dot_general | solution.py:159
  488.7 13.8 %gather_fusion = f32[128,2,64,256]{3,2,1,0:T(8,128)} fusion(f32[2,64,64,256]{3,2,0,1:T(8,128)} %bitcast_select_fusion, s32[1024]{0:T(1024)S(1)} %pad_clamp_fusion), kind=kCustom, calls=%fused_computation | custom fusion | bytes 33554944 | tf_op jit(solution)/shard_map/jit(_take)/gather | solution.py:163
  502.5 7.7 fusion.9
  510.2 369.0 %all_to_all.5 = f32[2,16,8,64,256]{4,3,1,0,2:T(8,128)S(1)} all-to-all(f32[2,16,8,64,256]{4,3,1,0,2:T(8,128)S(1)} %fusion.9), channel_id=1, replica_groups=mesh['tbit'=4,'box'=8] {'box'}, dimensions={2} | all-to-all | bytes 33554432 | tf_op jit(solution)/shard_map/all_to_all | solution.py:165
  879.2 6.2 copy.60
  (57 shorter events, 2.6 us)
Async XLA Ops:
  0.0 226.5 %copy-start = (s32[64,4,2,8]{0,3,2,1:T(8,128)S(1)}, s32[64,4,2,8]{0,3,2,1:T(8,128)}, u32[]{:S(2)}) copy-start(s32[64,4,2,8]{0,3,2,1:T(8,128)} %param.21) | copy-start | bytes 49156
  0.0 183.7 %collective-permute-start = (f32[64,2,64,256]{3,2,1,0:T(8,128)}, f32[64,2,64,256]{3,2,1,0:T(8,128)}, u32[]{:S(2)}, u32[]{:S(2)}) collective-permute-start(f32[64,2,64,256]{3,2,1,0:T(8,128)} %bitcast.74), channel_id=1, source_target_pairs={{0,16},{8,24},{16,0},{24,8},{1,17},{9,25},{17,1},{25,9},{2,18},{10... | collective-permute-start | bytes 25165832 | tf_op jit(solution)/shard_map/ppermute | solution.py:18
  183.7 31.2 %copy-start.4 = (f32[3,64,64]{2,1,0:T(8,128)S(1)}, f32[3,64,64]{2,1,0:T(8,128)}, u32[]{:S(2)}) copy-start(f32[3,64,64]{2,1,0:T(8,128)} %param.22) | copy-start | bytes 147460
  214.9 13.2 %copy-start.6 = (s32[64,2,1]{0,2,1:T(1,128)S(1)}, s32[64,2,1]{0,2,1:T(1,128)}, u32[]{:S(2)}) copy-start(s32[64,2,1]{0,2,1:T(1,128)} %param.20) | copy-start | bytes 1540
  214.9 14.6 %copy-start.5 = (s32[256,64]{0,1:T(8,128)S(1)}, s32[256,64]{0,1:T(8,128)}, u32[]{:S(2)}) copy-start(s32[256,64]{0,1:T(8,128)} %param.17) | copy-start | bytes 196612
  214.9 15.0 %copy-start.3 = (s32[512,64]{0,1:T(8,128)S(1)}, s32[512,64]{0,1:T(8,128)}, u32[]{:S(2)}) copy-start(s32[512,64]{0,1:T(8,128)} %param.18) | copy-start | bytes 393220
  215.0 15.7 %copy-start.2 = (s32[64,2,4,64]{3,2,1,0:T(4,128)S(1)}, s32[64,2,4,64]{3,2,1,0:T(4,128)}, u32[]{:S(2)}) copy-start(s32[64,2,4,64]{3,2,1,0:T(4,128)} %param.14) | copy-start | bytes 393220
  224.7 182.0 %collective-permute-start.1 = (f32[64,2,64,256]{3,2,1,0:T(8,128)}, f32[64,2,64,256]{3,2,1,0:T(8,128)}, u32[]{:S(2)}, u32[]{:S(2)}) collective-permute-start(f32[64,2,64,256]{3,2,1,0:T(8,128)} %select_bitcast_fusion), channel_id=1, source_target_pairs={{0,8},{8,0},{16,24},{24,16},{1,9},{9,1},{17,25},{25,17},{2,10},{10... | collective-permute-start | bytes 25165832 | tf_op jit(solution)/shard_map/ppermute | solution.py:18
  879.2 6.2 copy-start.1
where the time goes:
time: 886 us; the launch traced here: 885 us
  blocking collectives  369 us (42%)
  waiting for transfers between devices  353 us (40%)
  matrix products  123 us (14%)
  local copies, waits for them, and re-layouts  23.8 us (3%)
  other arithmetic  11.9 us (1%)
    all_to_all x1, blocking collectives, per_device(): lax.all_to_all(outgoing, 'box', split_axis=2, concat_axis=2, tiled=True)  369 us
    ppermute x2, waiting for transfers between devices, swapped(): return lax.ppermute(value, axis, pairs)  353 us
    dot_general x2, matrix products, partner_level(): jnp.einsum('ahcs,ahsn->ahcn', kernels, jnp.concatenate([mine_coeffs, arri...  62.5 us
    dot_general x1, matrix products, per_device(): jnp.einsum('acs,asn->acn', kernels, merged_two.reshape(parent_count, 2 *...  32.5 us
    dot_general x2, matrix products, partner_level(): merged = jnp.einsum('ij,ahjn->ahin', matrix, images, precision=highest)  18.2 us
  transfers between devices with their start and end apart: 2, of which 2 were waited for; matrix products, arithmetic and copies ran while one was open for 1% of the time, Pallas kernels for 0%

commit v1 on v0

v1 whole, which is shorter than its diff:
```python
import functools
import math

import jax
import jax.numpy as jnp
from jax import lax
from jax.experimental import pallas as pl
from jax.experimental.pallas import tpu as pltpu
from jax.sharding import PartitionSpec as P

NPTS = 1048576
PHASE_BITS = 20
CHUNKS = 8

SIN_TERMS = (
    1.0,
    -1.0 / 6.0,
    1.0 / 120.0,
    -1.0 / 5040.0,
    1.0 / 362880.0,
    -1.0 / 39916800.0,
    1.0 / 6227020800.0,
)


def swapped(value, axis, bit):
    mask = 2**bit
    pairs = [(source, source ^ mask) for source in range(lax.axis_size(axis))]
    return lax.ppermute(value, axis, pairs)


def slot_table(owner_row, box_count, capacity):
    parent_count = owner_row.shape[0]
    onehot = (owner_row[:, None] == jnp.arange(box_count, dtype=jnp.int32)[None, :]).astype(
        jnp.int32
    )
    earlier = jnp.cumsum(onehot, axis=0, dtype=jnp.int32) - onehot
    slot_of = jnp.sum(earlier * onehot, axis=1, dtype=jnp.int32)
    matches = (onehot.T[:, None, :] == 1) & (
        slot_of[None, None, :] == jnp.arange(capacity, dtype=jnp.int32)[None, :, None]
    )
    slot_parent = jnp.sum(
        jnp.where(matches, jnp.arange(parent_count, dtype=jnp.int32)[None, None, :], 0), axis=2
    )
    slot_used = jnp.any(matches, axis=2)
    return (slot_parent, slot_used)


def pick_slot(values, position):
    return lax.dynamic_index_in_dim(values, position, 2, keepdims=False)


def cos_kernel(targets, points):
    shift = 32 - PHASE_BITS
    phase = lax.shift_right_arithmetic(
        lax.shift_left(targets * points, jnp.int32(shift)), jnp.int32(shift)
    )
    offset = NPTS // 4 - jnp.abs(phase)
    y = offset.astype(jnp.float32) * jnp.float32(2.0 * math.pi / NPTS)
    square = y * y
    total = jnp.float32(SIN_TERMS[-1])
    for term in SIN_TERMS[-2::-1]:
        total = total * square + jnp.float32(term)
    return total * y


def split(value):
    high = value.astype(jnp.bfloat16)
    low = (value - high.astype(jnp.float32)).astype(jnp.bfloat16)
    return high, low


def product(left, right):
    rows = left.shape[0]
    left_high, left_low = split(left)
    right_high, right_low = split(right)
    both = jnp.dot(
        jnp.concatenate([left_high, left_low], axis=0),
        right_high,
        preferred_element_type=jnp.float32,
    )
    rest = jnp.dot(left_high, right_low, preferred_element_type=jnp.float32)
    return both[:rows] + both[rows:] + rest


def live(weights, rank):
    rows = lax.broadcasted_iota(jnp.int32, weights.shape, 0)
    return jnp.where(rows < rank, weights, 0.0)


def first_kernel(chunk, ranks, targets, points, matrix, mine, arrived, merged):
    step = pl.program_id(0)
    parents, boxes = mine.shape[0], mine.shape[1]
    for parent in range(parents):
        row = (chunk * pl.num_programs(0) + step) * parents + parent
        for box in range(boxes):
            kernel = cos_kernel(targets[parent], points[parent, box : box + 1, :])
            weights = live(product(matrix[...], kernel), ranks[row * boxes + box])
            stacked = jnp.concatenate([mine[parent, box], arrived[parent, box]], axis=0)
            merged[parent, box] = product(weights, stacked)


def later_kernel(
    chunk,
    ranks_second,
    ranks_third,
    targets_second,
    points_second,
    targets_third,
    points_third,
    matrices,
    mine,
    arrived,
    merged,
):
    step = pl.program_id(0)
    parents, boxes, rank_width = mine.shape[0], mine.shape[1], mine.shape[2]
    for parent in range(parents):
        row = (chunk * pl.num_programs(0) + step) * parents + parent
        seconds = []
        for box in range(boxes):
            kernel = cos_kernel(targets_second[parent], points_second[parent, box : box + 1, :])
            weights = live(product(matrices[0], kernel), ranks_second[row * boxes + box])
            stacked = jnp.concatenate([mine[parent, box], arrived[parent, box]], axis=0)
            seconds.append(product(weights, stacked))
        kernel = cos_kernel(targets_third[parent], points_third[parent])
        weights = []
        for child in range(2):
            part = product(matrices[1], kernel[child * rank_width : (child + 1) * rank_width])
            weights.append(live(part, ranks_third[row * 2 + child]))
        third = product(jnp.concatenate(weights, axis=0), jnp.concatenate(seconds, axis=0))
        for child in range(2):
            merged[parent, child] = third[child * rank_width : (child + 1) * rank_width]


def chunk_spec(shape, chunk, steps, per_step):
    block = (per_step,) + tuple(shape[1:])
    rest = (0,) * (len(shape) - 1)
    return pl.BlockSpec(block, lambda step, *_: (chunk * steps + step,) + rest)


def whole_spec(shape):
    rest = (0,) * len(shape)
    return pl.BlockSpec(tuple(shape), lambda step, *_: rest)


def first_level(chunk, count, ranks, targets, points, matrix, mine, arrived):
    per_step = 2
    steps = count // per_step
    return pl.pallas_call(
        functools.partial(first_kernel, chunk),
        grid_spec=pltpu.PrefetchScalarGridSpec(
            num_scalar_prefetch=1,
            grid=(steps,),
            in_specs=[
                chunk_spec(targets.shape, chunk, steps, per_step),
                chunk_spec(points.shape, chunk, steps, per_step),
                whole_spec(matrix.shape),
                chunk_spec(mine.shape, chunk, steps, per_step),
                chunk_spec(arrived.shape, 0, steps, per_step),
            ],
            out_specs=chunk_spec(arrived.shape, 0, steps, per_step),
        ),
        out_shape=jax.ShapeDtypeStruct(arrived.shape, jnp.float32),
        compiler_params=pltpu.CompilerParams(vmem_limit_bytes=32 * 1024 * 1024),
        name="first_level",
    )(ranks, targets, points, matrix, mine, arrived)


def later_levels(
    chunk, count, ranks, targets_second, points_second, targets_third, points_third, matrices, mine, arrived
):
    per_step = 2
    steps = count // per_step
    return pl.pallas_call(
        functools.partial(later_kernel, chunk),
        grid_spec=pltpu.PrefetchScalarGridSpec(
            num_scalar_prefetch=2,
            grid=(steps,),
            in_specs=[
                chunk_spec(targets_second.shape, chunk, steps, per_step),
                chunk_spec(points_second.shape, chunk, steps, per_step),
                chunk_spec(targets_third.shape, chunk, steps, per_step),
                chunk_spec(points_third.shape, chunk, steps, per_step),
                whole_spec(matrices.shape),
                chunk_spec(mine.shape, 0, steps, per_step),
                chunk_spec(arrived.shape, 0, steps, per_step),
            ],
            out_specs=chunk_spec(arrived.shape, 0, steps, per_step),
        ),
        out_shape=jax.ShapeDtypeStruct(arrived.shape, jnp.float32),
        compiler_params=pltpu.CompilerParams(vmem_limit_bytes=32 * 1024 * 1024),
        name="later_levels",
    )(
        ranks[0],
        ranks[1],
        targets_second,
        points_second,
        targets_third,
        points_third,
        matrices,
        mine,
        arrived,
    )


def per_device(
    coeffs,
    skeleton_first,
    skeleton_second,
    skeleton_third,
    checks_first,
    checks_second,
    checks_third,
    ranks_first,
    ranks_second,
    ranks_third,
    interpolants,
    owners,
):
    tbit_index = lax.axis_index("tbit")
    box_index = lax.axis_index("box")
    box_count = lax.axis_size("box")
    parent_count = coeffs.shape[0]
    rank_width = coeffs.shape[3]
    capacity = 2 * parent_count // box_count
    group_count = 2 * box_count
    local_boxes = 2 * box_index + jnp.arange(2, dtype=jnp.int32)[None, :, None]

    def targets_of(checks, per_parent, picked, width):
        boxes = per_parent * parent_count
        absolute = jnp.arange(boxes, dtype=jnp.int32)[:, None] * (NPTS // boxes) + checks
        mine = lax.dynamic_index_in_dim(
            absolute.reshape(parent_count, -1, width), picked, 1, keepdims=False
        )
        return mine[:, :, None]

    def first_points(slot):
        box = 4 * local_boxes + 2 * (slot % 2) + slot // 2
        return box * (NPTS // (4 * group_count)) + pick_slot(skeleton_first, slot)

    def second_points(slot):
        box = 2 * local_boxes + slot % 2
        return box * (NPTS // (2 * group_count)) + pick_slot(skeleton_second, slot)

    partner_high = jnp.bitwise_xor(tbit_index, 2)
    partner_low = jnp.bitwise_xor(tbit_index, 1)
    points_first = jnp.concatenate([first_points(tbit_index), first_points(partner_high)], axis=2)
    points_second = jnp.concatenate([second_points(tbit_index), second_points(partner_low)], axis=2)
    points_third = (
        local_boxes * (NPTS // group_count) + pick_slot(skeleton_third, tbit_index)
    ).reshape(parent_count, 1, 2 * rank_width)
    targets_first = targets_of(checks_first, 2, tbit_index // 2, rank_width)
    targets_second = targets_of(checks_second, 4, tbit_index, rank_width)
    targets_third = targets_of(checks_third, 8, tbit_index, 2 * rank_width)
    rank_one = ranks_first.reshape(-1)
    rank_two = ranks_second.reshape(-1)
    rank_three = lax.dynamic_index_in_dim(
        lax.dynamic_index_in_dim(ranks_third, tbit_index, 1, keepdims=False),
        box_index,
        2,
        keepdims=False,
    ).reshape(-1)

    mine = coeffs[:, :, 0]
    count = parent_count // CHUNKS
    arrived = []
    for chunk in range(CHUNKS):
        outgoing = mine[chunk * count : (chunk + 1) * count]
        if chunk > 0:
            outgoing, _ = lax.optimization_barrier((outgoing, arrived[-1]))
        arrived.append(swapped(outgoing, "tbit", 1))
    merged = []
    second_arrived = []
    for chunk in range(CHUNKS):
        first = first_level(
            chunk, count, rank_one, targets_first, points_first, interpolants[0], mine, arrived[chunk]
        )
        outgoing = first
        if chunk > 0:
            outgoing, _ = lax.optimization_barrier((outgoing, second_arrived[-1]))
        second_arrived.append(swapped(outgoing, "tbit", 0))
        merged.append(
            later_levels(
                chunk,
                count,
                (rank_two, rank_three),
                targets_second,
                points_second,
                targets_third,
                points_third,
                interpolants[1:],
                first,
                second_arrived[chunk],
            )
        )
    merged = jnp.concatenate(merged, axis=0)

    slot_parent, slot_used = slot_table(
        lax.dynamic_index_in_dim(owners, tbit_index, 0, keepdims=False), box_count, capacity
    )
    outgoing = jnp.take(jnp.swapaxes(merged, 0, 1), slot_parent.T, axis=1)
    outgoing = jnp.where(slot_used.T[None, :, :, None, None], outgoing, 0.0)
    switched = lax.all_to_all(outgoing, "box", split_axis=2, concat_axis=2, tiled=True)
    return switched[None, None]


def solution(mesh):
    return jax.shard_map(
        per_device,
        mesh=mesh,
        in_specs=(
            P(None, "box", "tbit", None, None),
            P(None, "box", None, None),
            P(None, "box", None, None),
            P(None, "box", None, None),
            P(),
            P(),
            P(),
            P(None, "box", "tbit"),
            P(None, "box", "tbit"),
            P(),
            P(),
            P(),
        ),
        out_specs=P("tbit", "box", None, None, None, None, None),
        check_vma=False,
    )
```

time: 886 us -> 673 us (0.76)
  waiting for transfers between devices: 353 us -> 114 us
  matrix products: 123 us -> 0 us
  Pallas kernels: 0 us -> 84.4 us
  local copies, waits for them, and re-layouts: 23.8 us -> 69.7 us
  starting transfers between devices: 4.73 us -> 22.1 us
    ppermute x2 -> x16, waiting for transfers between devices: 353 us -> 114 us  [swapped(): return lax.ppermute(value, axis, pairs)]
    dot_general x6 -> x0, matrix products: 123 us -> none  [the longest x2 62.5 us: partner_level(): jnp.einsum('ahcs,ahsn->ahcn', kernels, jnp.concatenate([mine_coeffs, arri...]
    pallas_call x0 -> x16, Pallas kernels: none -> 84.4 us  [the longest x8 48 us: later_levels(): pl.pallas_call(functools.partial(later_kernel, chunk), grid_spec=pltpu.Pr...]
    unnamed x15 -> x79, local copies, waits for them, and re-layouts: 0.88 us -> 23.3 us
    ppermute x2 -> x16, starting transfers between devices: 4.73 us -> 22.1 us  [swapped(): return lax.ppermute(value, axis, pairs)]
  transfers between devices with their start and end apart: 2 -> 16, of which waited for: 2 -> 12; matrix products, arithmetic and copies ran while one was open for 1% -> 4% of each run, Pallas kernels for 0% -> 12%
where the time goes in v1:
time: 673 us; the launch traced here: 672 us
  blocking collectives  368 us (55%)
  waiting for transfers between devices  114 us (17%)
  Pallas kernels  84.4 us (13%)
  local copies, waits for them, and re-layouts  69.7 us (10%)
  starting transfers between devices  22.1 us (3%)
  other arithmetic  12.6 us (2%)
    all_to_all x1, blocking collectives, per_device(): lax.all_to_all(outgoing, 'box', split_axis=2, concat_axis=2, tiled=True)  368 us
    ppermute x16, waiting for transfers between devices, swapped(): return lax.ppermute(value, axis, pairs)  114 us
    pallas_call x8, Pallas kernels, later_levels(): pl.pallas_call(functools.partial(later_kernel, chunk), grid_spec=pltpu.Pr...  48 us
    pallas_call x8, Pallas kernels, first_level(): pl.pallas_call(functools.partial(first_kernel, chunk), grid_spec=pltpu.Pr...  36.5 us
    unnamed x79, local copies, waits for them, and re-layouts  23.3 us
    ppermute x16, starting transfers between devices, swapped(): return lax.ppermute(value, axis, pairs)  22.1 us
    gather x1, local copies, waits for them, and re-layouts, per_device(): outgoing = jnp.take(jnp.swapaxes(merged, 0, 1), slot_parent.T, axis=1)  13.6 us
  transfers between devices with their start and end apart: 16, of which 12 were waited for; matrix products, arithmetic and copies ran while one was open for 4% of the time, Pallas kernels for 12%

profile of v1, /device:TPU:0, one launch (start us, length us, event | category | flops | bytes accessed | tf_op | source)
XLA Modules:
  0.0 671.9 jit_solution(5497314242462073594)
XLA Ops:
  0.0 6.6 slice_bitcast_fusion
  12.8 19.9 %collective-permute-done.arrived = f32[8,2,64,256]{3,2,1,0:T(8,128)S(1)} collective-permute-done((f32[8,2,64,256]{3,2,1,0:T(8,128)S(1)}, f32[8,2,64,256]{3,2,1,0:T(8,128)S(1)}, u32[]{:S(2)}, u32[]{:S(2)}) %collective-permute-start) | collective-permute-done | bytes 1048608 | tf_op jit(solution)/shard_map/ppermute | solution.py:29
  45.3 12.1 %collective-permute-done.2.arrived = f32[8,2,64,256]{3,2,1,0:T(8,128)} collective-permute-done((f32[8,2,64,256]{3,2,1,0:T(8,128)}, f32[8,2,64,256]{3,2,1,0:T(8,128)}, u32[]{:S(2)}, u32[]{:S(2)}) %collective-permute-start.2) | collective-permute-done | bytes 1048608 | tf_op jit(solution)/shard_map/ppermute | solution.py:29
  70.0 10.8 %collective-permute-done.4.arrived = f32[8,2,64,256]{3,2,1,0:T(8,128)S(1)} collective-permute-done((f32[8,2,64,256]{3,2,1,0:T(8,128)S(1)}, f32[8,2,64,256]{3,2,1,0:T(8,128)S(1)}, u32[]{:S(2)}, u32[]{:S(2)}) %collective-permute-start.4) | collective-permute-done | bytes 1048608 | tf_op jit(solution)/shard_map/ppermute | solution.py:29
  85.8 6.1 collective-permute-done.3.arrived
  93.4 10.8 %collective-permute-done.6.arrived = f32[8,2,64,256]{3,2,1,0:T(8,128)S(1)} collective-permute-done((f32[8,2,64,256]{3,2,1,0:T(8,128)S(1)}, f32[8,2,64,256]{3,2,1,0:T(8,128)S(1)}, u32[]{:S(2)}, u32[]{:S(2)}) %collective-permute-start.6) | collective-permute-done | bytes 1048608 | tf_op jit(solution)/shard_map/ppermute | solution.py:29
  109.1 6.0 collective-permute-done.5.arrived
  117.4 8.3 %collective-permute-done.8.arrived = f32[8,2,64,256]{3,2,1,0:T(8,128)S(1)} collective-permute-done((f32[8,2,64,256]{3,2,1,0:T(8,128)S(1)}, f32[8,2,64,256]{3,2,1,0:T(8,128)S(1)}, u32[]{:S(2)}, u32[]{:S(2)}) %collective-permute-start.8) | collective-permute-done | bytes 1048608 | tf_op jit(solution)/shard_map/ppermute | solution.py:29
  130.2 7.1 %collective-permute-done.7.arrived = f32[8,2,64,256]{3,2,1,0:T(8,128)S(1)} collective-permute-done((f32[8,2,64,256]{3,2,1,0:T(8,128)S(1)}, f32[8,2,64,256]{3,2,1,0:T(8,128)S(1)}, u32[]{:S(2)}, u32[]{:S(2)}) %collective-permute-start.7) | collective-permute-done | bytes 1048608 | tf_op jit(solution)/shard_map/ppermute | solution.py:29
  148.2 10.8 %collective-permute-done.10.arrived = f32[8,2,64,256]{3,2,1,0:T(8,128)} collective-permute-done((f32[8,2,64,256]{3,2,1,0:T(8,128)}, f32[8,2,64,256]{3,2,1,0:T(8,128)}, u32[]{:S(2)}, u32[]{:S(2)}) %collective-permute-start.10) | collective-permute-done | bytes 1048608 | tf_op jit(solution)/shard_map/ppermute | solution.py:29
  162.4 5.6 first_level.13.mine
  171.5 15.3 %collective-permute-done.12.arrived = f32[8,2,64,256]{3,2,1,0:T(8,128)} collective-permute-done((f32[8,2,64,256]{3,2,1,0:T(8,128)}, f32[8,2,64,256]{3,2,1,0:T(8,128)}, u32[]{:S(2)}, u32[]{:S(2)}) %collective-permute-start.12) | collective-permute-done | bytes 1048608 | tf_op jit(solution)/shard_map/ppermute | solution.py:29
  190.2 5.6 first_level.14.mine
  223.9 5.6 later_levels.8
  229.6 5.6 later_levels.9
  235.3 5.6 later_levels.10
  246.7 6.6 later_levels.12
  253.4 6.6 later_levels.13
  260.2 6.8 %later_levels.14 = f32[8,2,64,256]{3,2,1,0:T(8,128)S(1)} custom-call(s32[128]{0:T(128)S(1)} %reshape.169.ranks_second, s32[128]{0:T(128)S(1)} %reshape.170.ranks_third, s32[64,64,1]{2,1,0:T(8,128)S(1)} %copy-done.7, s32[64,2,128]{2,1,0:T(2,128)S(1)} %pad_add_fusion.points_second, s32[64,128,1]{2,1,0:T(8,128)S(1)} %copy-done.6, ...), custom_call_target="tpu_custom_call" | custom-call | tf_op jit(solution)/shard_map/later_levels/pallas_call | solution.py:175
  267.1 5.6 later_levels.15
  276.1 13.6 %gather_fusion = f32[128,2,64,256]{3,2,1,0:T(8,128)} fusion(f32[2,64,64,256]{3,2,0,1:T(8,128)} %bitcast.61, s32[1024]{0:T(1024)S(1)} %pad_clamp_fusion), kind=kCustom, calls=%fused_computation | custom fusion | bytes 33554944 | tf_op jit(solution)/shard_map/jit(_take)/gather | solution.py:302
  289.7 7.7 %fusion.1 = f32[2,16,8,64,256]{4,3,1,0,2:T(8,128)S(1)} fusion(f32[16,8,2,64,256]{4,3,2,1,0:T(8,128)} %bitcast.59, pred[16,8]{0,1:T(8,128)(4,1)S(1)} %bitcast.72, pred[16,8]{0,1:T(8,128)(4,1)S(1)} %compare_and_fusion), kind=kLoop, calls=%fused_computation.3 | loop fusion | flops 8388608 | bytes 33554688 | tf_op jit(solution)/shard_map/jit(_where)/select_n | solution.py:303
  297.4 368.3 %all_to_all.5 = f32[2,16,8,64,256]{4,3,1,0,2:T(8,128)S(1)} all-to-all(f32[2,16,8,64,256]{4,3,1,0,2:T(8,128)S(1)} %fusion.1), channel_id=1, replica_groups=mesh['tbit'=4,'box'=8] {'box'}, dimensions={2} | all-to-all | bytes 33554432 | tf_op jit(solution)/shard_map/all_to_all | solution.py:304
  665.7 6.2 copy.150
  (158 shorter events, 108.1 us)
Async XLA Ops:
  0.0 169.8 %copy-start = (s32[64,4,2,8]{0,3,2,1:T(8,128)S(1)}, s32[64,4,2,8]{0,3,2,1:T(8,128)}, u32[]{:S(2)}) copy-start(s32[64,4,2,8]{0,3,2,1:T(8,128)} %param.21) | copy-start | bytes 49156
  0.0 34.5 %copy-start.33 = (s32[64,2,1]{0,2,1:T(1,128)S(1)}, s32[64,2,1]{0,2,1:T(1,128)}, u32[]{:S(2)}) copy-start(s32[64,2,1]{0,2,1:T(1,128)} %param.19) | copy-start | bytes 1540
  6.6 26.1 %collective-permute-start = (f32[8,2,64,256]{3,2,1,0:T(8,128)S(1)}, f32[8,2,64,256]{3,2,1,0:T(8,128)S(1)}, u32[]{:S(2)}, u32[]{:S(2)}) collective-permute-start(f32[8,2,64,256]{3,2,1,0:T(8,128)S(1)} %get-tuple-element.40), channel_id=1, source_target_pairs={{0,16},{8,24},{16,0},{24,8},{1,17},{9,25},{17,1},{25,9},{2,18},{10... | collective-permute-start | bytes 3145736 | tf_op jit(solution)/shard_map/ppermute | solution.py:29
  32.7 24.7 %collective-permute-start.2 = (f32[8,2,64,256]{3,2,1,0:T(8,128)}, f32[8,2,64,256]{3,2,1,0:T(8,128)}, u32[]{:S(2)}, u32[]{:S(2)}) collective-permute-start(f32[8,2,64,256]{3,2,1,0:T(8,128)} %get-tuple-element.19), channel_id=1, source_target_pairs={{0,16},{8,24},{16,0},{24,8},{1,17},{9,25},{17,1},{25,9},{2,18},{10... | collective-permute-start | bytes 3145736 | tf_op jit(solution)/shard_map/ppermute | solution.py:29
  43.7 37.1 %copy-start.26 = (f32[8,2,64,256]{3,2,1,0:T(8,128)S(1)}, f32[8,2,64,256]{3,2,1,0:T(8,128)}, u32[]{:S(2)}) copy-start(f32[8,2,64,256]{3,2,1,0:T(8,128)} %get-tuple-element.23) | copy-start | bytes 3145732
  43.7 23.8 %collective-permute-start.1 = (f32[8,2,64,256]{3,2,1,0:T(8,128)S(1)}, f32[8,2,64,256]{3,2,1,0:T(8,128)S(1)}, u32[]{:S(2)}, u32[]{:S(2)}) collective-permute-start(f32[8,2,64,256]{3,2,1,0:T(8,128)S(1)} %first_level.8.mine), channel_id=1, source_target_pairs={{0,8},{8,0},{16,24},{24,16},{1,9},{9,1},{17,25},{25,17},{2,10},{10... | collective-permute-start | bytes 3145736 | tf_op jit(solution)/shard_map/ppermute | solution.py:29
  57.4 23.4 %collective-permute-start.4 = (f32[8,2,64,256]{3,2,1,0:T(8,128)S(1)}, f32[8,2,64,256]{3,2,1,0:T(8,128)S(1)}, u32[]{:S(2)}, u32[]{:S(2)}) collective-permute-start(f32[8,2,64,256]{3,2,1,0:T(8,128)S(1)} %copy-done.27), channel_id=1, source_target_pairs={{0,16},{8,24},{16,0},{24,8},{1,17},{9,25},{17,1},{25,9},{2,18},{10... | collective-permute-start | bytes 3145736 | tf_op jit(solution)/shard_map/ppermute | solution.py:29
  63.6 45.5 %copy-start.8 = (f32[8,2,64,256]{3,2,1,0:T(8,128)}, f32[8,2,64,256]{3,2,1,0:T(8,128)S(1)}, u32[]{:S(2)}) copy-start(f32[8,2,64,256]{3,2,1,0:T(8,128)S(1)} %first_level.9.mine) | copy-start | bytes 3145732
  63.6 40.5 %copy-start.25 = (f32[8,2,64,256]{3,2,1,0:T(8,128)S(1)}, f32[8,2,64,256]{3,2,1,0:T(8,128)}, u32[]{:S(2)}) copy-start(f32[8,2,64,256]{3,2,1,0:T(8,128)} %get-tuple-element.25) | copy-start | bytes 3145732
  68.5 23.3 %collective-permute-start.3 = (f32[8,2,64,256]{3,2,1,0:T(8,128)S(1)}, f32[8,2,64,256]{3,2,1,0:T(8,128)S(1)}, u32[]{:S(2)}, u32[]{:S(2)}) collective-permute-start(f32[8,2,64,256]{3,2,1,0:T(8,128)S(1)} %first_level.9.mine), channel_id=1, source_target_pairs={{0,8},{8,0},{16,24},{24,16},{1,9},{9,1},{17,25},{25,17},{2,10},{10... | collective-permute-start | bytes 3145736 | tf_op jit(solution)/shard_map/ppermute | solution.py:29
  80.8 23.3 %collective-permute-start.6 = (f32[8,2,64,256]{3,2,1,0:T(8,128)S(1)}, f32[8,2,64,256]{3,2,1,0:T(8,128)S(1)}, u32[]{:S(2)}, u32[]{:S(2)}) collective-permute-start(f32[8,2,64,256]{3,2,1,0:T(8,128)S(1)} %copy-done.26), channel_id=1, source_target_pairs={{0,16},{8,24},{16,0},{24,8},{1,17},{9,25},{17,1},{25,9},{2,18},{10... | collective-permute-start | bytes 3145736 | tf_op jit(solution)/shard_map/ppermute | solution.py:29
  85.8 44.4 %copy-start.10 = (f32[8,2,64,256]{3,2,1,0:T(8,128)}, f32[8,2,64,256]{3,2,1,0:T(8,128)S(1)}, u32[]{:S(2)}) copy-start(f32[8,2,64,256]{3,2,1,0:T(8,128)S(1)} %first_level.10.mine) | copy-start | bytes 3145732
  91.9 23.3 %collective-permute-start.5 = (f32[8,2,64,256]{3,2,1,0:T(8,128)S(1)}, f32[8,2,64,256]{3,2,1,0:T(8,128)S(1)}, u32[]{:S(2)}, u32[]{:S(2)}) collective-permute-start(f32[8,2,64,256]{3,2,1,0:T(8,128)S(1)} %first_level.10.mine), channel_id=1, source_target_pairs={{0,8},{8,0},{16,24},{24,16},{1,9},{9,1},{17,25},{25,17},{2,10},{10... | collective-permute-start | bytes 3145736 | tf_op jit(solution)/shard_map/ppermute | solution.py:29
  104.1 21.6 %collective-permute-start.8 = (f32[8,2,64,256]{3,2,1,0:T(8,128)S(1)}, f32[8,2,64,256]{3,2,1,0:T(8,128)S(1)}, u32[]{:S(2)}, u32[]{:S(2)}) collective-permute-start(f32[8,2,64,256]{3,2,1,0:T(8,128)S(1)} %copy-done.25), channel_id=1, source_target_pairs={{0,16},{8,24},{16,0},{24,8},{1,17},{9,25},{17,1},{25,9},{2,18},{10... | collective-permute-start | bytes 3145736 | tf_op jit(solution)/shard_map/ppermute | solution.py:29
  109.1 31.9 %copy-start.29 = (s32[512,64]{0,1:T(8,128)S(1)}, s32[512,64]{0,1:T(8,128)}, u32[]{:S(2)}) copy-start(s32[512,64]{0,1:T(8,128)} %param.18) | copy-start | bytes 393220
  115.2 22.1 %collective-permute-start.7 = (f32[8,2,64,256]{3,2,1,0:T(8,128)S(1)}, f32[8,2,64,256]{3,2,1,0:T(8,128)S(1)}, u32[]{:S(2)}, u32[]{:S(2)}) collective-permute-start(f32[8,2,64,256]{3,2,1,0:T(8,128)S(1)} %first_level.11.mine), channel_id=1, source_target_pairs={{0,8},{8,0},{16,24},{24,16},{1,9},{9,1},{17,25},{25,17},{2,10},{10... | collective-permute-start | bytes 3145736 | tf_op jit(solution)/shard_map/ppermute | solution.py:29
  138.3 29.8 %collective-permute-start.9 = (f32[8,2,64,256]{3,2,1,0:T(8,128)}, f32[8,2,64,256]{3,2,1,0:T(8,128)}, u32[]{:S(2)}, u32[]{:S(2)}) collective-permute-start(f32[8,2,64,256]{3,2,1,0:T(8,128)} %first_level.12.mine), channel_id=1, source_target_pairs={{0,8},{8,0},{16,24},{24,16},{1,9},{9,1},{17,25},{25,17},{2,10},{10... | collective-permute-start | bytes 3145736 | tf_op jit(solution)/shard_map/ppermute | solution.py:29
  139.8 19.3 %collective-permute-start.10 = (f32[8,2,64,256]{3,2,1,0:T(8,128)}, f32[8,2,64,256]{3,2,1,0:T(8,128)}, u32[]{:S(2)}, u32[]{:S(2)}) collective-permute-start(f32[8,2,64,256]{3,2,1,0:T(8,128)} %get-tuple-element.27), channel_id=1, source_target_pairs={{0,16},{8,24},{16,0},{24,8},{1,17},{9,25},{17,1},{25,9},{2,18},{10... | collective-permute-start | bytes 3145736 | tf_op jit(solution)/shard_map/ppermute | solution.py:29
  168.1 34.9 %copy-start.28 = (s32[64,2,64]{2,1,0:T(2,128)S(1)}, s32[64,2,64]{2,1,0:T(2,128)}, u32[]{:S(2)}) copy-start(s32[64,2,64]{2,1,0:T(2,128)} %get-tuple-element.45) | copy-start | bytes 98308
  168.1 27.7 %collective-permute-start.11 = (f32[8,2,64,256]{3,2,1,0:T(8,128)}, f32[8,2,64,256]{3,2,1,0:T(8,128)}, u32[]{:S(2)}, u32[]{:S(2)}) collective-permute-start(f32[8,2,64,256]{3,2,1,0:T(8,128)} %first_level.13.mine), channel_id=1, source_target_pairs={{0,8},{8,0},{16,24},{24,16},{1,9},{9,1},{17,25},{25,17},{2,10},{10... | collective-permute-start | bytes 3145736 | tf_op jit(solution)/shard_map/ppermute | solution.py:29
  168.6 18.2 %collective-permute-start.12 = (f32[8,2,64,256]{3,2,1,0:T(8,128)}, f32[8,2,64,256]{3,2,1,0:T(8,128)}, u32[]{:S(2)}, u32[]{:S(2)}) collective-permute-start(f32[8,2,64,256]{3,2,1,0:T(8,128)} %get-tuple-element.29), channel_id=1, source_target_pairs={{0,16},{8,24},{16,0},{24,8},{1,17},{9,25},{17,1},{25,9},{2,18},{10... | collective-permute-start | bytes 3145736 | tf_op jit(solution)/shard_map/ppermute | solution.py:29
  195.8 26.7 %collective-permute-start.13 = (f32[8,2,64,256]{3,2,1,0:T(8,128)}, f32[8,2,64,256]{3,2,1,0:T(8,128)}, u32[]{:S(2)}, u32[]{:S(2)}) collective-permute-start(f32[8,2,64,256]{3,2,1,0:T(8,128)} %first_level.14.mine), channel_id=1, source_target_pairs={{0,8},{8,0},{16,24},{24,16},{1,9},{9,1},{17,25},{25,17},{2,10},{10... | collective-permute-start | bytes 3145736 | tf_op jit(solution)/shard_map/ppermute | solution.py:29
  197.1 16.8 %collective-permute-start.14 = (f32[8,2,64,256]{3,2,1,0:T(8,128)}, f32[8,2,64,256]{3,2,1,0:T(8,128)}, u32[]{:S(2)}, u32[]{:S(2)}) collective-permute-start(f32[8,2,64,256]{3,2,1,0:T(8,128)} %get-tuple-element.31), channel_id=1, source_target_pairs={{0,16},{8,24},{16,0},{24,8},{1,17},{9,25},{17,1},{25,9},{2,18},{10... | collective-permute-start | bytes 3145736 | tf_op jit(solution)/shard_map/ppermute | solution.py:29
  222.5 44.6 %collective-permute-start.15 = (f32[8,2,64,256]{3,2,1,0:T(8,128)S(1)}, f32[8,2,64,256]{3,2,1,0:T(8,128)S(1)}, u32[]{:S(2)}, u32[]{:S(2)}) collective-permute-start(f32[8,2,64,256]{3,2,1,0:T(8,128)S(1)} %first_level.15.mine), channel_id=1, source_target_pairs={{0,8},{8,0},{16,24},{24,16},{1,9},{9,1},{17,25},{25,17},{2,10},{10... | collective-permute-start | bytes 3145736 | tf_op jit(solution)/shard_map/ppermute | solution.py:29
  (26 other events, 220.2 us)

commit v2 on v1

--- a/solution.py
+++ b/solution.py
@@ -11,6 +11,9 @@
 NPTS = 1048576
 PHASE_BITS = 20
 CHUNKS = 8
+LANES = 8
+LAG = 2
+STATIC_ROUNDS = 11
 
 SIN_TERMS = (
     1.0,
@@ -104,6 +107,7 @@
     chunk,
     ranks_second,
     ranks_third,
+    place,
     targets_second,
     points_second,
     targets_third,
@@ -111,8 +115,9 @@
     matrices,
     mine,
     arrived,
-    merged,
+    *pool,
 ):
+    merged = pool[-1]
     step = pl.program_id(0)
     parents, boxes, rank_width = mine.shape[0], mine.shape[1], mine.shape[2]
     for parent in range(parents):
@@ -168,14 +173,31 @@
 
 
 def later_levels(
-    chunk, count, ranks, targets_second, points_second, targets_third, points_third, matrices, mine, arrived
+    chunk,
+    count,
+    ranks,
+    place,
+    targets_second,
+    points_second,
+    targets_third,
+    points_third,
+    matrices,
+    mine,
+    arrived,
+    pool_shape,
+    pool,
 ):
     per_step = 2
     steps = count // per_step
+    parents = targets_second.shape[0]
+
+    def pool_block(step, ranks_second, ranks_third, place):
+        return (place[0] * (parents // per_step) + chunk * steps + step, 0, 0, 0)
+
     return pl.pallas_call(
         functools.partial(later_kernel, chunk),
         grid_spec=pltpu.PrefetchScalarGridSpec(
-            num_scalar_prefetch=2,
+            num_scalar_prefetch=3,
             grid=(steps,),
             in_specs=[
                 chunk_spec(targets_second.shape, chunk, steps, per_step),
@@ -185,15 +207,18 @@
                 whole_spec(matrices.shape),
                 chunk_spec(mine.shape, 0, steps, per_step),
                 chunk_spec(arrived.shape, 0, steps, per_step),
-            ],
-            out_specs=chunk_spec(arrived.shape, 0, steps, per_step),
+            ]
+            + [pl.BlockSpec(memory_space=pl.ANY)] * len(pool),
+            out_specs=pl.BlockSpec((per_step,) + pool_shape[1:], pool_block),
         ),
-        out_shape=jax.ShapeDtypeStruct(arrived.shape, jnp.float32),
+        out_shape=jax.ShapeDtypeStruct(pool_shape, jnp.float32),
+        input_output_aliases={10: 0} if pool else {},
         compiler_params=pltpu.CompilerParams(vmem_limit_bytes=32 * 1024 * 1024),
         name="later_levels",
     )(
         ranks[0],
         ranks[1],
+        place,
         targets_second,
         points_second,
         targets_third,
@@ -201,7 +226,299 @@
         matrices,
         mine,
         arrived,
-    )
+        *pool,
+    )
+
+
+def plan_kernel(chips, lanes, limit, capacity, chunks, owners, place, table, slots, rounds, own, ahead, used):
+    parents = owners.shape[0]
+    count = parents // chunks
+    z = place[0]
+    span = limit * lanes
+
+    def clear(index, carry):
+        table[index] = -1
+        return carry
+
+    lax.fori_loop(0, 4 * span, clear, 0)
+    for box in range(2 * chips):
+        used[box] = 0
+
+    def take_slot(parent, carry):
+        owner = owners[parent]
+        slots[parent] = owner * capacity + used[owner]
+        used[owner] = used[owner] + 1
+        return carry
+
+    lax.fori_loop(0, parents, take_slot, 0)
+    width = chips * parents
+    pairs = [(chip, goal) for chip in range(1, chips) for goal in range(chip + 1, chips)]
+    last = []
+    for direction in range(2):
+
+        def true_chip(chip):
+            return chip if direction == 0 else chips - 1 - chip
+
+        total = 0
+        for box in range(2 * chips):
+            hops = true_chip(box // 2)
+            total = total + used[box] * (hops * (hops + 1) // 2)
+
+        def one_round(state):
+            step, left, ready, own_head, head, tail, older = state
+            ready, own_head, head, tail = list(ready), list(own_head), list(head), list(tail)
+
+            def add_own(index, ready):
+                parent = jnp.minimum(step * count + index, parents - 1)
+                goal = owners[parent] // 2
+                goal = goal if direction == 0 else chips - 1 - goal
+                fresh = []
+                for chip in range(1, chips):
+                    here = (goal == chip) & (step < chunks)
+
+                    @pl.when(here)
+                    def _(chip=chip):
+                        own[chip * parents + ready[chip]] = parent
+
+                    fresh.append(ready[chip] + here.astype(jnp.int32))
+                return (ready[0],) + tuple(fresh)
+
+            for index in range(count):
+                ready = add_own(index, ready)
+            seen = older[0]
+            newer = list(older[1:])
+            sent = jnp.int32(0)
+            for chip in range(chips - 1):
+                for lane in range(lanes):
+                    code, taken = jnp.int32(-1), jnp.bool_(False)
+                    for goal in range(chips - 1, chip, -1):
+                        which = (chip, goal)
+                        if which in pairs:
+                            place_of = pairs.index(which)
+                            can = jnp.logical_not(taken) & (head[place_of] < seen[place_of])
+                            value = ahead[place_of * width + jnp.minimum(head[place_of], width - 1)]
+                            code = jnp.where(can, value, code)
+                            head[place_of] = head[place_of] + can.astype(jnp.int32)
+                            taken = taken | can
+                            if (chip + 1, goal) in pairs:
+                                onward(ahead, pairs.index((chip + 1, goal)), width, tail, value, can)
+                        queue = chip * chips + goal
+                        can = jnp.logical_not(taken) & (own_head[queue] < ready[goal])
+                        value = own[goal * parents + jnp.minimum(own_head[queue], parents - 1)]
+                        value = true_chip(chip) * parents + value
+                        code = jnp.where(can, value, code)
+                        own_head[queue] = own_head[queue] + can.astype(jnp.int32)
+                        taken = taken | can
+                        if (chip + 1, goal) in pairs:
+                            onward(ahead, pairs.index((chip + 1, goal)), width, tail, value, can)
+                    sent = sent + taken.astype(jnp.int32)
+                    spot = direction * span + step * lanes + lane
+
+                    @pl.when(z == true_chip(chip))
+                    def _(code=code, spot=spot):
+                        table[spot] = code
+
+                    @pl.when(z == true_chip(chip + 1))
+                    def _(code=code, spot=spot):
+                        table[2 * span + spot] = code
+
+            newer.append(tuple(tail))
+            return (
+                step + 1,
+                left - sent,
+                tuple(ready),
+                tuple(own_head),
+                tuple(head),
+                tuple(tail),
+                tuple(newer),
+            )
+
+        zero = jnp.int32(0)
+        none = (zero,) * len(pairs)
+        state = lax.while_loop(
+            lambda state: (state[1] > 0) & (state[0] < limit),
+            one_round,
+            (zero, jnp.int32(total), (zero,) * chips, (zero,) * (chips * chips), none, none, (none,) * LAG),
+        )
+        last.append(state[0])
+    rounds[0] = jnp.maximum(last[0], last[1])
+
+
+def onward(ahead, place_of, width, tail, value, can):
+    @pl.when(can)
+    def _(spot=tail[place_of]):
+        ahead[place_of * width + spot] = value
+
+    tail[place_of] = tail[place_of] + can.astype(jnp.int32)
+
+
+def plan_switch(owner_row, place, chips, capacity):
+    parents = owner_row.shape[0]
+    limit = round_limit(parents)
+    smem = pl.BlockSpec(memory_space=pltpu.SMEM)
+    return pl.pallas_call(
+        functools.partial(plan_kernel, chips, LANES, limit, capacity, CHUNKS),
+        in_specs=[smem, smem],
+        out_specs=[smem, smem, smem],
+        out_shape=[
+            jax.ShapeDtypeStruct((4 * limit * LANES,), jnp.int32),
+            jax.ShapeDtypeStruct((parents,), jnp.int32),
+            jax.ShapeDtypeStruct((1,), jnp.int32),
+        ],
+        scratch_shapes=[
+            pltpu.SMEM((chips * parents,), jnp.int32),
+            pltpu.SMEM((chips * chips * chips * parents,), jnp.int32),
+            pltpu.SMEM((2 * chips,), jnp.int32),
+        ],
+        name="plan_switch",
+    )(owner_row, place)
+
+
+def round_limit(parents):
+    return 5 * parents // LANES
+
+
+def round_kernel(
+    lanes,
+    limit,
+    parents,
+    capacity,
+    receives,
+    fresh,
+    sends,
+    table,
+    slots,
+    place,
+    now,
+    *refs,
+):
+    received = refs[: 2 * receives]
+    refs = refs[2 * receives + 3 :]
+    pool, out, stage = refs[:3]
+    outgoing = refs[3 : 3 + 2 * sends]
+    sems = refs[-1]
+    z, core = place[0], place[1]
+    span = limit * lanes
+
+    def to_home(index, code, source, begin):
+        parent = lax.rem(jnp.maximum(code, 0), parents)
+        from_chip = lax.div(jnp.maximum(code, 0), parents)
+        spot = slots[parent]
+        owner, slot = lax.div(spot, capacity), lax.rem(spot, capacity)
+        here = (code >= 0) & (lax.div(owner, 2) == z)
+
+        @pl.when(here & (lax.rem(owner, 2) == core))
+        def _():
+            copy = pltpu.make_async_copy(source, out.at[:, slot, from_chip, core], sems.at[index])
+            copy.start() if begin else copy.wait()
+
+        @pl.when(here & (lax.rem(owner, 2) != core))
+        def _():
+            copy = pltpu.make_async_copy(source, stage.at[:, slot, from_chip], sems.at[index])
+            copy.start() if begin else copy.wait()
+
+        return here
+
+    def take_in(begin):
+        index = 0
+        for back in range(receives):
+            for direction in range(2):
+                for lane in range(lanes):
+                    step = now[0] - LAG + back
+                    code = table[(2 + direction) * span + jnp.maximum(step, 0) * lanes + lane]
+                    code = jnp.where(step >= 0, code, -1)
+                    source = received[2 * back + direction].at[lane]
+                    here = to_home(index, code, source, begin)
+
+                    @pl.when((code >= 0) & jnp.logical_not(here))
+                    def _(code=code, source=source, index=index):
+                        copy = pltpu.make_async_copy(source, pool.at[code], sems.at[index])
+                        copy.start() if begin else copy.wait()
+
+                    index += 1
+        for member in range(fresh):
+            code = z * parents + now[0] * fresh + member
+            to_home(index, code, pool.at[code], begin)
+            index += 1
+
+    def send(begin):
+        for direction in range(2):
+            for lane in range(lanes):
+                code = table[direction * span + now[0] * lanes + lane]
+
+                @pl.when(code >= 0)
+                def _(code=code, direction=direction, lane=lane):
+                    copy = pltpu.make_async_copy(
+                        pool.at[code], outgoing[direction].at[lane], sems.at[direction * lanes + lane]
+                    )
+                    copy.start() if begin else copy.wait()
+
+    take_in(True)
+    take_in(False)
+    if sends:
+        send(True)
+        send(False)
+
+
+def switch_round(plan, place, now, received, state, fresh, sends):
+    table, slots = plan
+    pool, out, stage = state
+    parents = slots.shape[0]
+    capacity = out.shape[1]
+    receives = len(received)
+    flat = [array for pair in received for array in pair]
+    anywhere = pl.BlockSpec(memory_space=pl.ANY)
+    lane_shape = jax.ShapeDtypeStruct((LANES,) + pool.shape[1:], jnp.float32)
+    first = 4 + len(flat)
+    results = pl.pallas_call(
+        functools.partial(
+            round_kernel, LANES, round_limit(parents), parents, capacity, receives, fresh, int(sends)
+        ),
+        grid_spec=pltpu.PrefetchScalarGridSpec(
+            num_scalar_prefetch=4,
+            grid=(),
+            in_specs=[anywhere] * (len(flat) + 3),
+            out_specs=[anywhere] * (3 + 2 * int(sends)),
+            scratch_shapes=[pltpu.SemaphoreType.DMA((2 * LANES * max(receives, 1) + fresh,))],
+        ),
+        out_shape=[jax.ShapeDtypeStruct(array.shape, array.dtype) for array in state]
+        + [lane_shape] * (2 * int(sends)),
+        input_output_aliases={first: 0, first + 1: 1, first + 2: 2},
+        name="switch_round",
+    )(table, slots, place, now, *flat, *state)
+    return tuple(results[:3]), tuple(results[3:])
+
+
+def join_kernel(place, arrived, out_before, out, sem):
+    copy = pltpu.make_async_copy(arrived, out.at[:, :, :, 1 - place[1]], sem)
+    copy.start()
+    copy.wait()
+
+
+def join_cores(place, arrived, out):
+    anywhere = pl.BlockSpec(memory_space=pl.ANY)
+    return pl.pallas_call(
+        join_kernel,
+        grid_spec=pltpu.PrefetchScalarGridSpec(
+            num_scalar_prefetch=1,
+            grid=(),
+            in_specs=[anywhere, anywhere],
+            out_specs=anywhere,
+            scratch_shapes=[pltpu.SemaphoreType.DMA],
+        ),
+        out_shape=jax.ShapeDtypeStruct(out.shape, out.dtype),
+        input_output_aliases={2: 0},
+        name="join_cores",
+    )(place, arrived, out)
+
+
+def along_line(value, chips, up):
+    pairs = []
+    for chip in range(chips - 1):
+        for core in range(2):
+            low, high = 2 * chip + core, 2 * (chip + 1) + core
+            pairs.append((low, high) if up else (high, low))
+    return lax.ppermute(value, "box", pairs)
 
 
 def per_device(
@@ -264,15 +581,28 @@
 
     mine = coeffs[:, :, 0]
     count = parent_count // CHUNKS
+    chips = box_count // 2
+    networked = chips <= 4
+    place = jnp.stack([box_index // 2, box_index % 2]).astype(jnp.int32)
+    owner_row = lax.dynamic_index_in_dim(owners, tbit_index, 0, keepdims=False)
+    width = coeffs.shape[-1]
+    if networked:
+        table, slots, rounds = plan_switch(owner_row, place, chips, capacity)
+        pool_shape = (chips * parent_count, 2, rank_width, width)
+    else:
+        place = jnp.zeros_like(place)
+        pool_shape = (parent_count, 2, rank_width, width)
+
     arrived = []
     for chunk in range(CHUNKS):
         outgoing = mine[chunk * count : (chunk + 1) * count]
         if chunk > 0:
             outgoing, _ = lax.optimization_barrier((outgoing, arrived[-1]))
         arrived.append(swapped(outgoing, "tbit", 1))
-    merged = []
+
     second_arrived = []
-    for chunk in range(CHUNKS):
+
+    def levels(chunk, pool):
         first = first_level(
             chunk, count, rank_one, targets_first, points_first, interpolants[0], mine, arrived[chunk]
         )
@@ -280,29 +610,69 @@
         if chunk > 0:
             outgoing, _ = lax.optimization_barrier((outgoing, second_arrived[-1]))
         second_arrived.append(swapped(outgoing, "tbit", 0))
-        merged.append(
-            later_levels(
-                chunk,
-                count,
-                (rank_two, rank_three),
-                targets_second,
-                points_second,
-                targets_third,
-                points_third,
-                interpolants[1:],
-                first,
-                second_arrived[chunk],
-            )
+        return later_levels(
+            chunk,
+            count,
+            (rank_two, rank_three),
+            place,
+            targets_second,
+            points_second,
+            targets_third,
+            points_third,
+            interpolants[1:],
+            first,
+            second_arrived[chunk],
+            pool_shape,
+            pool,
         )
-    merged = jnp.concatenate(merged, axis=0)
-
-    slot_parent, slot_used = slot_table(
-        lax.dynamic_index_in_dim(owners, tbit_index, 0, keepdims=False), box_count, capacity
-    )
-    outgoing = jnp.take(jnp.swapaxes(merged, 0, 1), slot_parent.T, axis=1)
-    outgoing = jnp.where(slot_used.T[None, :, :, None, None], outgoing, 0.0)
-    switched = lax.all_to_all(outgoing, "box", split_axis=2, concat_axis=2, tiled=True)
-    return switched[None, None]
+
+    if not networked:
+        pool = levels(0, ())
+        for chunk in range(1, CHUNKS):
+            pool = levels(chunk, (pool,))
+        slot_parent, slot_used = slot_table(owner_row, box_count, capacity)
+        outgoing = jnp.take(jnp.swapaxes(pool, 0, 1), slot_parent.T, axis=1)
+        outgoing = jnp.where(slot_used.T[None, :, :, None, None], outgoing, 0.0)
+        switched = lax.all_to_all(outgoing, "box", split_axis=2, concat_axis=2, tiled=True)
+        return switched[None, None]
+
+    out = jnp.zeros((2, capacity, chips, 2, rank_width, width), jnp.float32)
+    stage = jnp.zeros((2, capacity, chips, rank_width, width), jnp.float32)
+    state = (None, out, stage)
+    plan = (table, slots)
+    received = []
+
+    def exchange(packed):
+        return (along_line(packed[0], chips, True), along_line(packed[1], chips, False))
+
+    for step in range(STATIC_ROUNDS):
+        fresh = 0
+        if step < CHUNKS:
+            state = (levels(step, state[:1] if step else ()),) + state[1:]
+            fresh = count
+        now = jnp.full((1,), step, jnp.int32)
+        oldest = received[step - LAG : step - LAG + 1] if step >= LAG else []
+        state, packed = switch_round(plan, place, now, oldest, state, fresh, True)
+        received.append(exchange(packed))
+
+    most = jnp.maximum(lax.pmax(rounds[0], "tbit"), STATIC_ROUNDS)
+
+    def more(carry):
+        return carry[0] < most
+
+    def again(carry):
+        step, state, waiting = carry
+        state, packed = switch_round(plan, place, step[None], waiting[:1], state, 0, True)
+        return (step + 1, state, waiting[1:] + (exchange(packed),))
+
+    step, state, waiting = lax.while_loop(
+        more, again, (jnp.int32(STATIC_ROUNDS), state, tuple(received[-LAG:]))
+    )
+    state, _ = switch_round(plan, place, step[None], waiting, state, 0, False)
+    _, out, stage = state
+    crossed = lax.ppermute(stage, "box", [(box, box ^ 1) for box in range(box_count)])
+    out = join_cores(place, crossed, out)
+    return out.reshape(1, 1, 2, capacity, box_count, rank_width, width)
 
 
 def solution(mesh):

time: 673 us -> 1730 us (2.57)
  Pallas kernels: 84.4 us -> 855 us
  starting transfers between devices: 22.1 us -> 637 us
  blocking collectives: 368 us -> 6.22 us
  local copies, waits for them, and re-layouts: 69.7 us -> 102 us
    pallas_call x0 -> x15, Pallas kernels: none -> 758 us  [the longest x13 482 us: switch_round(): pl.pallas_call(functools.partial(round_kernel, LANES, round_limit(parents...]
    ppermute x0 -> x25, starting transfers between devices: none -> 600 us  [the longest x24 600 us: along_line(): return lax.ppermute(value, 'box', pairs)]
    all_to_all x1 -> x0, blocking collectives: 368 us -> none  [per_device(): lax.all_to_all(outgoing, 'box', split_axis=2, concat_axis=2, tiled=True)]
    ppermute x0 -> x25, waiting for transfers between devices: none -> 51 us  [the longest x24 37.5 us: along_line(): return lax.ppermute(value, 'box', pairs)]
    ppermute x16, waiting for transfers between devices: 114 us -> 65.4 us  [swapped(): return lax.ppermute(value, axis, pairs)]
    unnamed x79 -> x80, local copies, waits for them, and re-layouts: 23.3 us -> 60.6 us
  transfers between devices with their start and end apart: 16 -> 41, of which waited for: 12 -> 12; matrix products, arithmetic and copies ran while one was open for 4% -> 2% of each run, Pallas kernels for 12% -> 33%
where the time goes in v2:
time: 1730 us; the launch traced here: 1720 us
  Pallas kernels  855 us (49%)
  starting transfers between devices  637 us (37%)
  waiting for transfers between devices  116 us (7%)
  local copies, waits for them, and re-layouts  102 us (6%)
    ppermute x24, starting transfers between devices, along_line(): return lax.ppermute(value, 'box', pairs)  600 us
    pallas_call x13, Pallas kernels, switch_round(): pl.pallas_call(functools.partial(round_kernel, LANES, round_limit(parents...  482 us
    pallas_call x1, Pallas kernels, join_cores(): pl.pallas_call(join_kernel, grid_spec=pltpu.PrefetchScalarGridSpec(num_sc...  256 us
    ppermute x16, waiting for transfers between devices, swapped(): return lax.ppermute(value, axis, pairs)  65.4 us
    unnamed x80, local copies, waits for them, and re-layouts  60.6 us
    pallas_call x8, Pallas kernels, later_levels(): pl.pallas_call(functools.partial(later_kernel, chunk), grid_spec=pltpu.Pr...  57.6 us
    pallas_call x8, Pallas kernels, first_level(): pl.pallas_call(functools.partial(first_kernel, chunk), grid_spec=pltpu.Pr...  39.3 us
    ppermute x24, waiting for transfers between devices, along_line(): return lax.ppermute(value, 'box', pairs)  37.5 us
  transfers between devices with their start and end apart: 41, of which 12 were waited for; matrix products, arithmetic and copies ran while one was open for 2% of the time, Pallas kernels for 33%

profile of v2, /device:TPU:0, one launch (start us, length us, event | category | flops | bytes accessed | tf_op | source)
XLA Modules:
  0.0 1720.7 jit_solution(7747058910239135907)
XLA Ops:
  9.7 23.0 %collective-permute-done.2.arrived = f32[8,2,64,256]{3,2,1,0:T(8,128)S(1)} collective-permute-done((f32[8,2,64,256]{3,2,1,0:T(8,128)S(1)}, f32[8,2,64,256]{3,2,1,0:T(8,128)S(1)}, u32[]{:S(2)}, u32[]{:S(2)}) %collective-permute-start.2) | collective-permute-done | bytes 1048608 | tf_op jit(solution)/shard_map/ppermute | solution.py:32
  137.4 20.5 %plan_switch.1 = (s32[1280]{0:T(1024)S(1)}, s32[64]{0:T(128)S(1)}, s32[1]{0:T(128)}) custom-call(s32[64]{0:T(128)} %fusion.owners, s32[2]{0:T(128)S(1)} %pad_add_fusion.2.place), custom_call_target="tpu_custom_call" | custom-call | tf_op jit(solution)/shard_map/plan_switch/pallas_call | solution.py:359
  195.5 34.9 %switch_round.13 = (f32[256,2,64,256]{3,2,1,0:T(8,128)}, f32[2,16,4,2,64,256]{5,4,3,2,1,0:T(8,128)}, f32[2,16,4,64,256]{4,3,2,1,0:T(8,128)}, f32[8,2,64,256]{3,2,1,0:T(8,128)}, f32[8,2,64,256]{3,2,1,0:T(8,128)}) custom-call(s32[1280]{0:T(1024)S(1)} %get-tuple-element.370.table, ...), custom_call_target="tpu_custom_call", output_to_operand_aliasing={{0}: (4, {}), {1}: (5, {}), {2}: (6, {})} | custom-call | tf_op jit(solution)/shard_map/switch_round/pallas_call | solution.py:473
  247.3 34.9 %switch_round.14 = (f32[256,2,64,256]{3,2,1,0:T(8,128)}, f32[2,16,4,2,64,256]{5,4,3,2,1,0:T(8,128)}, f32[2,16,4,64,256]{4,3,2,1,0:T(8,128)}, f32[8,2,64,256]{3,2,1,0:T(8,128)}, f32[8,2,64,256]{3,2,1,0:T(8,128)}) custom-call(s32[1280]{0:T(1024)S(1)} %get-tuple-element.370.table, ...), custom_call_target="tpu_custom_call", output_to_operand_aliasing={{0}: (4, {}), {1}: (5, {}), {2}: (6, {})} | custom-call | tf_op jit(solution)/shard_map/switch_round/pallas_call | solution.py:473
  309.6 39.1 %switch_round.15 = (f32[256,2,64,256]{3,2,1,0:T(8,128)}, f32[2,16,4,2,64,256]{5,4,3,2,1,0:T(8,128)}, f32[2,16,4,64,256]{4,3,2,1,0:T(8,128)}, f32[8,2,64,256]{3,2,1,0:T(8,128)}, f32[8,2,64,256]{3,2,1,0:T(8,128)}) custom-call(s32[1280]{0:T(1024)S(1)} %get-tuple-element.370.table, ...), custom_call_target="tpu_custom_call", output_to_operand_aliasing={{0}: (6, {}), {1}: (7, {}), {2}: (8, {})} | custom-call | tf_op jit(solution)/shard_map/switch_round/pallas_call | solution.py:473
  359.8 64.8 %collective-permute-start.10 = (f32[8,2,64,256]{3,2,1,0:T(8,128)}, f32[8,2,64,256]{3,2,1,0:T(8,128)}, u32[]{:S(2)}, u32[]{:S(2)}) collective-permute-start(f32[8,2,64,256]{3,2,1,0:T(8,128)} %get-tuple-element.168), channel_id=1, source_target_pairs={{0,2},{1,3},{2,4},{3,5},{4,6},{5,7},{8,10},{9,11},{10,12},{11,13},... | collective-permute-start | bytes 3145736 | tf_op jit(solution)/shard_map/ppermute | solution.py:521
  425.9 47.0 %switch_round.16 = (f32[256,2,64,256]{3,2,1,0:T(8,128)}, f32[2,16,4,2,64,256]{5,4,3,2,1,0:T(8,128)}, f32[2,16,4,64,256]{4,3,2,1,0:T(8,128)}, f32[8,2,64,256]{3,2,1,0:T(8,128)}, f32[8,2,64,256]{3,2,1,0:T(8,128)}) custom-call(s32[1280]{0:T(1024)S(1)} %get-tuple-element.370.table, ...), custom_call_target="tpu_custom_call", output_to_operand_aliasing={{0}: (6, {}), {1}: (7, {}), {2}: (8, {})} | custom-call | tf_op jit(solution)/shard_map/switch_round/pallas_call | solution.py:473
  473.0 49.0 %collective-permute-start.24 = (f32[8,2,64,256]{3,2,1,0:T(8,128)}, f32[8,2,64,256]{3,2,1,0:T(8,128)}, u32[]{:S(2)}, u32[]{:S(2)}) collective-permute-start(f32[8,2,64,256]{3,2,1,0:T(8,128)} %get-tuple-element.188), channel_id=1, source_target_pairs={{0,2},{1,3},{2,4},{3,5},{4,6},{5,7},{8,10},{9,11},{10,12},{11,13},... | collective-permute-start | bytes 3145736 | tf_op jit(solution)/shard_map/ppermute | solution.py:521
  553.5 58.9 %switch_round.17 = (f32[256,2,64,256]{3,2,1,0:T(8,128)}, f32[2,16,4,2,64,256]{5,4,3,2,1,0:T(8,128)}, f32[2,16,4,64,256]{4,3,2,1,0:T(8,128)}, f32[8,2,64,256]{3,2,1,0:T(8,128)}, f32[8,2,64,256]{3,2,1,0:T(8,128)}) custom-call(s32[1280]{0:T(1024)S(1)} %get-tuple-element.370.table, ...), custom_call_target="tpu_custom_call", output_to_operand_aliasing={{0}: (6, {}), {1}: (7, {}), {2}: (8, {})} | custom-call | tf_op jit(solution)/shard_map/switch_round/pallas_call | solution.py:473
  612.4 68.7 %collective-permute-start.18 = (f32[8,2,64,256]{3,2,1,0:T(8,128)}, f32[8,2,64,256]{3,2,1,0:T(8,128)}, u32[]{:S(2)}, u32[]{:S(2)}) collective-permute-start(f32[8,2,64,256]{3,2,1,0:T(8,128)} %get-tuple-element.182), channel_id=1, source_target_pairs={{0,2},{1,3},{2,4},{3,5},{4,6},{5,7},{8,10},{9,11},{10,12},{11,13},... | collective-permute-start | bytes 3145736 | tf_op jit(solution)/shard_map/ppermute | solution.py:521
  693.5 51.0 %switch_round.18 = (f32[256,2,64,256]{3,2,1,0:T(8,128)}, f32[2,16,4,2,64,256]{5,4,3,2,1,0:T(8,128)}, f32[2,16,4,64,256]{4,3,2,1,0:T(8,128)}, f32[8,2,64,256]{3,2,1,0:T(8,128)}, f32[8,2,64,256]{3,2,1,0:T(8,128)}) custom-call(s32[1280]{0:T(1024)S(1)} %get-tuple-element.370.table, ...), custom_call_target="tpu_custom_call", output_to_operand_aliasing={{0}: (6, {}), {1}: (7, {}), {2}: (8, {})} | custom-call | tf_op jit(solution)/shard_map/switch_round/pallas_call | solution.py:473
  744.5 72.8 %collective-permute-start.28 = (f32[8,2,64,256]{3,2,1,0:T(8,128)}, f32[8,2,64,256]{3,2,1,0:T(8,128)}, u32[]{:S(2)}, u32[]{:S(2)}) collective-permute-start(f32[8,2,64,256]{3,2,1,0:T(8,128)} %get-tuple-element.198), channel_id=1, source_target_pairs={{0,2},{1,3},{2,4},{3,5},{4,6},{5,7},{8,10},{9,11},{10,12},{11,13},... | collective-permute-start | bytes 3145736 | tf_op jit(solution)/shard_map/ppermute | solution.py:521
  846.9 66.9 %switch_round.19 = (f32[256,2,64,256]{3,2,1,0:T(8,128)}, f32[2,16,4,2,64,256]{5,4,3,2,1,0:T(8,128)}, f32[2,16,4,64,256]{4,3,2,1,0:T(8,128)}, f32[8,2,64,256]{3,2,1,0:T(8,128)}, f32[8,2,64,256]{3,2,1,0:T(8,128)}) custom-call(s32[1280]{0:T(1024)S(1)} %get-tuple-element.370.table, ...), custom_call_target="tpu_custom_call", output_to_operand_aliasing={{0}: (6, {}), {1}: (7, {}), {2}: (8, {})} | custom-call | tf_op jit(solution)/shard_map/switch_round/pallas_call | solution.py:473
  913.8 68.8 %collective-permute-start.26 = (f32[8,2,64,256]{3,2,1,0:T(8,128)}, f32[8,2,64,256]{3,2,1,0:T(8,128)}, u32[]{:S(2)}, u32[]{:S(2)}) collective-permute-start(f32[8,2,64,256]{3,2,1,0:T(8,128)} %get-tuple-element.196), channel_id=1, source_target_pairs={{0,2},{1,3},{2,4},{3,5},{4,6},{5,7},{8,10},{9,11},{10,12},{11,13},... | collective-permute-start | bytes 3145736 | tf_op jit(solution)/shard_map/ppermute | solution.py:521
  993.4 58.9 %switch_round.20 = (f32[256,2,64,256]{3,2,1,0:T(8,128)}, f32[2,16,4,2,64,256]{5,4,3,2,1,0:T(8,128)}, f32[2,16,4,64,256]{4,3,2,1,0:T(8,128)}, f32[8,2,64,256]{3,2,1,0:T(8,128)}, f32[8,2,64,256]{3,2,1,0:T(8,128)}) custom-call(s32[1280]{0:T(1024)S(1)} %get-tuple-element.370.table, ...), custom_call_target="tpu_custom_call", output_to_operand_aliasing={{0}: (6, {}), {1}: (7, {}), {2}: (8, {})} | custom-call | tf_op jit(solution)/shard_map/switch_round/pallas_call | solution.py:473
  1052.3 59.9 %collective-permute-start.34 = (f32[8,2,64,256]{3,2,1,0:T(8,128)}, f32[8,2,64,256]{3,2,1,0:T(8,128)S(1)}, u32[]{:S(2)}, u32[]{:S(2)}) collective-permute-start(f32[8,2,64,256]{3,2,1,0:T(8,128)} %get-tuple-element.210), channel_id=1, source_target_pairs={{0,2},{1,3},{2,4},{3,5},{4,6},{5,7},{8,10},{9,11},{10,12},{11,13},... | collective-permute-start | bytes 3145736 | tf_op jit(solution)/shard_map/ppermute | solution.py:521
  1113.6 33.9 %switch_round.21 = (f32[256,2,64,256]{3,2,1,0:T(8,128)}, f32[2,16,4,2,64,256]{5,4,3,2,1,0:T(8,128)}, f32[2,16,4,64,256]{4,3,2,1,0:T(8,128)}, f32[8,2,64,256]{3,2,1,0:T(8,128)}, f32[8,2,64,256]{3,2,1,0:T(8,128)}) custom-call(s32[1280]{0:T(1024)S(1)} %get-tuple-element.370.table, ...), custom_call_target="tpu_custom_call", output_to_operand_aliasing={{0}: (6, {}), {1}: (7, {}), {2}: (8, {})} | custom-call | tf_op jit(solution)/shard_map/switch_round/pallas_call | solution.py:473
  1147.5 76.9 %collective-permute-start.32 = (f32[8,2,64,256]{3,2,1,0:T(8,128)}, f32[8,2,64,256]{3,2,1,0:T(8,128)S(1)}, u32[]{:S(2)}, u32[]{:S(2)}) collective-permute-start(f32[8,2,64,256]{3,2,1,0:T(8,128)} %get-tuple-element.208), channel_id=1, source_target_pairs={{0,2},{1,3},{2,4},{3,5},{4,6},{5,7},{8,10},{9,11},{10,12},{11,13},... | collective-permute-start | bytes 3145736 | tf_op jit(solution)/shard_map/ppermute | solution.py:521
  1227.1 26.0 %switch_round.22 = (f32[256,2,64,256]{3,2,1,0:T(8,128)}, f32[2,16,4,2,64,256]{5,4,3,2,1,0:T(8,128)}, f32[2,16,4,64,256]{4,3,2,1,0:T(8,128)}, f32[8,2,64,256]{3,2,1,0:T(8,128)}, f32[8,2,64,256]{3,2,1,0:T(8,128)}) custom-call(s32[1280]{0:T(1024)S(1)} %get-tuple-element.370.table, ...), custom_call_target="tpu_custom_call", output_to_operand_aliasing={{0}: (6, {}), {1}: (7, {}), {2}: (8, {})} | custom-call | tf_op jit(solution)/shard_map/switch_round/pallas_call | solution.py:473
  1254.1 18.0 %switch_round.23 = (f32[256,2,64,256]{3,2,1,0:T(8,128)}, f32[2,16,4,2,64,256]{5,4,3,2,1,0:T(8,128)}, f32[2,16,4,64,256]{4,3,2,1,0:T(8,128)}, f32[8,2,64,256]{3,2,1,0:T(8,128)}, f32[8,2,64,256]{3,2,1,0:T(8,128)}) custom-call(s32[1280]{0:T(1024)S(1)} %get-tuple-element.370.table, ...), custom_call_target="tpu_custom_call", output_to_operand_aliasing={{0}: (6, {}), {1}: (7, {}), {2}: (8, {})} | custom-call | tf_op jit(solution)/shard_map/switch_round/pallas_call | solution.py:473
  1272.1 80.1 %collective-permute-start.38 = (f32[8,2,64,256]{3,2,1,0:T(8,128)}, f32[8,2,64,256]{3,2,1,0:T(8,128)S(1)}, u32[]{:S(2)}, u32[]{:S(2)}) collective-permute-start(f32[8,2,64,256]{3,2,1,0:T(8,128)} %get-tuple-element.223), channel_id=1, source_target_pairs={{0,2},{1,3},{2,4},{3,5},{4,6},{5,7},{8,10},{9,11},{10,12},{11,13},... | collective-permute-start | bytes 3145736 | tf_op jit(solution)/shard_map/ppermute | solution.py:521
  1353.5 20.2 %collective-permute-start.36 = (f32[8,2,64,256]{3,2,1,0:T(8,128)}, f32[8,2,64,256]{3,2,1,0:T(8,128)S(1)}, u32[]{:S(2)}, u32[]{:S(2)}) collective-permute-start(f32[8,2,64,256]{3,2,1,0:T(8,128)} %get-tuple-element.221), channel_id=1, source_target_pairs={{0,2},{1,3},{2,4},{3,5},{4,6},{5,7},{8,10},{9,11},{10,12},{11,13},... | collective-permute-start | bytes 3145736 | tf_op jit(solution)/shard_map/ppermute | solution.py:521
  1404.9 35.9 %while.22 = (s32[]{:T(128)}, f32[256,2,64,256]{3,2,1,0:T(8,128)}, f32[2,16,4,2,64,256]{5,4,3,2,1,0:T(8,128)}, f32[2,16,4,64,256]{4,3,2,1,0:T(8,128)}, f32[8,2,64...) while((s32[]{:T(128)}, f32[256,2,64,256]{3,2,1,0:T(8,128)}, ...), condition=%wide.region_2.3_spmd, body=%wide.region_1.2_spmd.sunk | while | flops 2 | bytes 16777420 | solution.py:668
  1464.7 255.8 %join_cores.1 = f32[2,16,4,2,64,256]{5,4,3,2,1,0:T(8,128)} custom-call(s32[2]{0:T(128)S(1)} %get-tuple-element.419, f32[2,16,4,64,256]{4,3,2,1,0:T(8,128)} %collective-permute-done.40.arrived, f32[2,16,4,2,64,256]{5,4,3,2,1,0:T(8,128)} %get-tuple-element.235.out_before), custom_call_target="tpu_custom_call", output_to_operand_aliasing={{}: (2, {})} | custom-call | tf_op jit(solution)/shard_map/join_cores/pallas_call | solution.py:500
  (216 shorter events, 389.0 us)
Async XLA Ops:
  128.6 159.1 %collective-permute-start.20 = (f32[8,2,64,256]{3,2,1,0:T(8,128)}, f32[8,2,64,256]{3,2,1,0:T(8,128)}, u32[]{:S(2)}, u32[]{:S(2)}) collective-permute-start(f32[8,2,64,256]{3,2,1,0:T(8,128)} %get-tuple-element.184), channel_id=1, source_target_pairs={{0,16},{8,24},{16,0},{24,8},{1,17},{9,25},{17,1},{25,9},{2,18},{10... | collective-permute-start | bytes 3145736 | tf_op jit(solution)/shard_map/ppermute | solution.py:32
  181.8 126.5 %collective-permute-start.15 = (f32[8,2,64,256]{3,2,1,0:T(8,128)}, f32[8,2,64,256]{3,2,1,0:T(8,128)}, u32[]{:S(2)}, u32[]{:S(2)}) collective-permute-start(f32[8,2,64,256]{3,2,1,0:T(8,128)} %first_level.11.mine), channel_id=1, source_target_pairs={{0,8},{8,0},{16,24},{24,16},{1,9},{9,1},{17,25},{25,17},{2,10},{10... | collective-permute-start | bytes 3145736 | tf_op jit(solution)/shard_map/ppermute | solution.py:32
  230.4 78.5 %collective-permute-start.4 = (f32[8,2,64,256]{3,2,1,0:T(8,128)}, f32[8,2,64,256]{3,2,1,0:T(8,128)}, u32[]{:S(2)}, u32[]{:S(2)}) collective-permute-start(f32[8,2,64,256]{3,2,1,0:T(8,128)} %get-tuple-element.156), channel_id=1, source_target_pairs={{0,2},{1,3},{2,4},{3,5},{4,6},{5,7},{8,10},{9,11},{10,12},{11,13},... | collective-permute-start | bytes 3145736 | tf_op jit(solution)/shard_map/ppermute | solution.py:521
  282.2 142.4 %collective-permute-start.16 = (f32[8,2,64,256]{3,2,1,0:T(8,128)}, f32[8,2,64,256]{3,2,1,0:T(8,128)}, u32[]{:S(2)}, u32[]{:S(2)}) collective-permute-start(f32[8,2,64,256]{3,2,1,0:T(8,128)} %get-tuple-element.174), channel_id=1, source_target_pairs={{0,2},{1,3},{2,4},{3,5},{4,6},{5,7},{8,10},{9,11},{10,12},{11,13},... | collective-permute-start | bytes 3145736 | tf_op jit(solution)/shard_map/ppermute | solution.py:521
  287.7 138.3 %collective-permute-start.17 = (f32[8,2,64,256]{3,2,1,0:T(8,128)}, f32[8,2,64,256]{3,2,1,0:T(8,128)}, u32[]{:S(2)}, u32[]{:S(2)}) collective-permute-start(f32[8,2,64,256]{3,2,1,0:T(8,128)} %get-tuple-element.175), channel_id=1, source_target_pairs={{2,0},{3,1},{4,2},{5,3},{6,4},{7,5},{10,8},{11,9},{12,10},{13,11},... | collective-permute-start | bytes 3145736 | tf_op jit(solution)/shard_map/ppermute | solution.py:521
  308.3 224.8 %collective-permute-start.21 = (f32[8,2,64,256]{3,2,1,0:T(8,128)}, f32[8,2,64,256]{3,2,1,0:T(8,128)}, u32[]{:S(2)}, u32[]{:S(2)}) collective-permute-start(f32[8,2,64,256]{3,2,1,0:T(8,128)} %get-tuple-element.185), channel_id=1, source_target_pairs={{0,16},{8,24},{16,0},{24,8},{1,17},{9,25},{17,1},{25,9},{2,18},{10... | collective-permute-start | bytes 3145736 | tf_op jit(solution)/shard_map/ppermute | solution.py:32
  308.9 234.4 %collective-permute-start.22 = (f32[8,2,64,256]{3,2,1,0:T(8,128)S(1)}, f32[8,2,64,256]{3,2,1,0:T(8,128)}, u32[]{:S(2)}, u32[]{:S(2)}) collective-permute-start(f32[8,2,64,256]{3,2,1,0:T(8,128)S(1)} %first_level.14.mine), channel_id=1, source_target_pairs={{0,8},{8,0},{16,24},{24,16},{1,9},{9,1},{17,25},{25,17},{2,10},{10... | collective-permute-start | bytes 3145736 | tf_op jit(solution)/shard_map/ppermute | solution.py:32
  359.8 185.5 %collective-permute-start.10 = (f32[8,2,64,256]{3,2,1,0:T(8,128)}, f32[8,2,64,256]{3,2,1,0:T(8,128)}, u32[]{:S(2)}, u32[]{:S(2)}) collective-permute-start(f32[8,2,64,256]{3,2,1,0:T(8,128)} %get-tuple-element.168), channel_id=1, source_target_pairs={{0,2},{1,3},{2,4},{3,5},{4,6},{5,7},{8,10},{9,11},{10,12},{11,13},... | collective-permute-start | bytes 3145736 | tf_op jit(solution)/shard_map/ppermute | solution.py:521
  424.6 128.8 %collective-permute-start.11 = (f32[8,2,64,256]{3,2,1,0:T(8,128)}, f32[8,2,64,256]{3,2,1,0:T(8,128)}, u32[]{:S(2)}, u32[]{:S(2)}) collective-permute-start(f32[8,2,64,256]{3,2,1,0:T(8,128)} %get-tuple-element.169), channel_id=1, source_target_pairs={{2,0},{3,1},{4,2},{5,3},{6,4},{7,5},{10,8},{11,9},{12,10},{13,11},... | collective-permute-start | bytes 3145736 | tf_op jit(solution)/shard_map/ppermute | solution.py:521
  473.0 208.2 %collective-permute-start.24 = (f32[8,2,64,256]{3,2,1,0:T(8,128)}, f32[8,2,64,256]{3,2,1,0:T(8,128)}, u32[]{:S(2)}, u32[]{:S(2)}) collective-permute-start(f32[8,2,64,256]{3,2,1,0:T(8,128)} %get-tuple-element.188), channel_id=1, source_target_pairs={{0,2},{1,3},{2,4},{3,5},{4,6},{5,7},{8,10},{9,11},{10,12},{11,13},... | collective-permute-start | bytes 3145736 | tf_op jit(solution)/shard_map/ppermute | solution.py:521
  542.1 151.4 %collective-permute-start.25 = (f32[8,2,64,256]{3,2,1,0:T(8,128)}, f32[8,2,64,256]{3,2,1,0:T(8,128)}, u32[]{:S(2)}, u32[]{:S(2)}) collective-permute-start(f32[8,2,64,256]{3,2,1,0:T(8,128)} %get-tuple-element.189), channel_id=1, source_target_pairs={{2,0},{3,1},{4,2},{5,3},{6,4},{7,5},{10,8},{11,9},{12,10},{13,11},... | collective-permute-start | bytes 3145736 | tf_op jit(solution)/shard_map/ppermute | solution.py:521
  543.4 273.9 %collective-permute-start.30 = (f32[8,2,64,256]{3,2,1,0:T(8,128)}, f32[8,2,64,256]{3,2,1,0:T(8,128)}, u32[]{:S(2)}, u32[]{:S(2)}) collective-permute-start(f32[8,2,64,256]{3,2,1,0:T(8,128)} %get-tuple-element.200), channel_id=1, source_target_pairs={{0,16},{8,24},{16,0},{24,8},{1,17},{9,25},{17,1},{25,9},{2,18},{10... | collective-permute-start | bytes 3145736 | tf_op jit(solution)/shard_map/ppermute | solution.py:32
  545.3 280.1 %collective-permute-start.23 = (f32[8,2,64,256]{3,2,1,0:T(8,128)}, f32[8,2,64,256]{3,2,1,0:T(8,128)}, u32[]{:S(2)}, u32[]{:S(2)}) collective-permute-start(f32[8,2,64,256]{3,2,1,0:T(8,128)} %first_level.13.mine), channel_id=1, source_target_pairs={{0,8},{8,0},{16,24},{24,16},{1,9},{9,1},{17,25},{25,17},{2,10},{10... | collective-permute-start | bytes 3145736 | tf_op jit(solution)/shard_map/ppermute | solution.py:32
  612.4 234.5 %collective-permute-start.18 = (f32[8,2,64,256]{3,2,1,0:T(8,128)}, f32[8,2,64,256]{3,2,1,0:T(8,128)}, u32[]{:S(2)}, u32[]{:S(2)}) collective-permute-start(f32[8,2,64,256]{3,2,1,0:T(8,128)} %get-tuple-element.182), channel_id=1, source_target_pairs={{0,2},{1,3},{2,4},{3,5},{4,6},{5,7},{8,10},{9,11},{10,12},{11,13},... | collective-permute-start | bytes 3145736 | tf_op jit(solution)/shard_map/ppermute | solution.py:521
  681.1 165.8 %collective-permute-start.19 = (f32[8,2,64,256]{3,2,1,0:T(8,128)}, f32[8,2,64,256]{3,2,1,0:T(8,128)}, u32[]{:S(2)}, u32[]{:S(2)}) collective-permute-start(f32[8,2,64,256]{3,2,1,0:T(8,128)} %get-tuple-element.183), channel_id=1, source_target_pairs={{2,0},{3,1},{4,2},{5,3},{6,4},{7,5},{10,8},{11,9},{12,10},{13,11},... | collective-permute-start | bytes 3145736 | tf_op jit(solution)/shard_map/ppermute | solution.py:521
  744.5 248.9 %collective-permute-start.28 = (f32[8,2,64,256]{3,2,1,0:T(8,128)}, f32[8,2,64,256]{3,2,1,0:T(8,128)}, u32[]{:S(2)}, u32[]{:S(2)}) collective-permute-start(f32[8,2,64,256]{3,2,1,0:T(8,128)} %get-tuple-element.198), channel_id=1, source_target_pairs={{0,2},{1,3},{2,4},{3,5},{4,6},{5,7},{8,10},{9,11},{10,12},{11,13},... | collective-permute-start | bytes 3145736 | tf_op jit(solution)/shard_map/ppermute | solution.py:521
  825.5 158.4 %collective-permute-start.31 = (f32[8,2,64,256]{3,2,1,0:T(8,128)S(1)}, f32[8,2,64,256]{3,2,1,0:T(8,128)}, u32[]{:S(2)}, u32[]{:S(2)}) collective-permute-start(f32[8,2,64,256]{3,2,1,0:T(8,128)S(1)} %first_level.15.mine), channel_id=1, source_target_pairs={{0,8},{8,0},{16,24},{24,16},{1,9},{9,1},{17,25},{25,17},{2,10},{10... | collective-permute-start | bytes 3145736 | tf_op jit(solution)/shard_map/ppermute | solution.py:32
  845.6 147.8 %collective-permute-start.29 = (f32[8,2,64,256]{3,2,1,0:T(8,128)}, f32[8,2,64,256]{3,2,1,0:T(8,128)}, u32[]{:S(2)}, u32[]{:S(2)}) collective-permute-start(f32[8,2,64,256]{3,2,1,0:T(8,128)} %get-tuple-element.199), channel_id=1, source_target_pairs={{2,0},{3,1},{4,2},{5,3},{6,4},{7,5},{10,8},{11,9},{12,10},{13,11},... | collective-permute-start | bytes 3145736 | tf_op jit(solution)/shard_map/ppermute | solution.py:521
  913.8 199.7 %collective-permute-start.26 = (f32[8,2,64,256]{3,2,1,0:T(8,128)}, f32[8,2,64,256]{3,2,1,0:T(8,128)}, u32[]{:S(2)}, u32[]{:S(2)}) collective-permute-start(f32[8,2,64,256]{3,2,1,0:T(8,128)} %get-tuple-element.196), channel_id=1, source_target_pairs={{0,2},{1,3},{2,4},{3,5},{4,6},{5,7},{8,10},{9,11},{10,12},{11,13},... | collective-permute-start | bytes 3145736 | tf_op jit(solution)/shard_map/ppermute | solution.py:521
  982.6 131.0 %collective-permute-start.27 = (f32[8,2,64,256]{3,2,1,0:T(8,128)}, f32[8,2,64,256]{3,2,1,0:T(8,128)}, u32[]{:S(2)}, u32[]{:S(2)}) collective-permute-start(f32[8,2,64,256]{3,2,1,0:T(8,128)} %get-tuple-element.197), channel_id=1, source_target_pairs={{2,0},{3,1},{4,2},{5,3},{6,4},{7,5},{10,8},{11,9},{12,10},{13,11},... | collective-permute-start | bytes 3145736 | tf_op jit(solution)/shard_map/ppermute | solution.py:521
  1052.3 173.4 %collective-permute-start.34 = (f32[8,2,64,256]{3,2,1,0:T(8,128)}, f32[8,2,64,256]{3,2,1,0:T(8,128)S(1)}, u32[]{:S(2)}, u32[]{:S(2)}) collective-permute-start(f32[8,2,64,256]{3,2,1,0:T(8,128)} %get-tuple-element.210), channel_id=1, source_target_pairs={{0,2},{1,3},{2,4},{3,5},{4,6},{5,7},{8,10},{9,11},{10,12},{11,13},... | collective-permute-start | bytes 3145736 | tf_op jit(solution)/shard_map/ppermute | solution.py:521
  1112.3 113.5 %collective-permute-start.35 = (f32[8,2,64,256]{3,2,1,0:T(8,128)}, f32[8,2,64,256]{3,2,1,0:T(8,128)S(1)}, u32[]{:S(2)}, u32[]{:S(2)}) collective-permute-start(f32[8,2,64,256]{3,2,1,0:T(8,128)} %get-tuple-element.211), channel_id=1, source_target_pairs={{2,0},{3,1},{4,2},{5,3},{6,4},{7,5},{10,8},{11,9},{12,10},{13,11},... | collective-permute-start | bytes 3145736 | tf_op jit(solution)/shard_map/ppermute | solution.py:521
  1147.5 105.5 %collective-permute-start.32 = (f32[8,2,64,256]{3,2,1,0:T(8,128)}, f32[8,2,64,256]{3,2,1,0:T(8,128)S(1)}, u32[]{:S(2)}, u32[]{:S(2)}) collective-permute-start(f32[8,2,64,256]{3,2,1,0:T(8,128)} %get-tuple-element.208), channel_id=1, source_target_pairs={{0,2},{1,3},{2,4},{3,5},{4,6},{5,7},{8,10},{9,11},{10,12},{11,13},... | collective-permute-start | bytes 3145736 | tf_op jit(solution)/shard_map/ppermute | solution.py:521
  1272.1 109.7 %collective-permute-start.38 = (f32[8,2,64,256]{3,2,1,0:T(8,128)}, f32[8,2,64,256]{3,2,1,0:T(8,128)S(1)}, u32[]{:S(2)}, u32[]{:S(2)}) collective-permute-start(f32[8,2,64,256]{3,2,1,0:T(8,128)} %get-tuple-element.223), channel_id=1, source_target_pairs={{0,2},{1,3},{2,4},{3,5},{4,6},{5,7},{8,10},{9,11},{10,12},{11,13},... | collective-permute-start | bytes 3145736 | tf_op jit(solution)/shard_map/ppermute | solution.py:521
  (55 other events, 1273.0 us)

commit v3 on v2

v3 whole, which is shorter than its diff:
```python
import functools
import math

import jax
import jax.numpy as jnp
from jax import lax
from jax.experimental import pallas as pl
from jax.experimental.pallas import tpu as pltpu
from jax.sharding import PartitionSpec as P

NPTS = 1048576
PHASE_BITS = 20
CHUNKS = 8
LANES = 8
LAG = 2
STATIC_ROUNDS = 12
PER_STEP = 4
VMEM_BYTES = 32 * 1024 * 1024
CODE_SHIFT = 16
SLOT_SHIFT = 16
POINTS_SECOND = 2
POINTS_THIRD = 4
TARGETS_LOW = 5
TARGETS_HIGH = 6

SIN_TERMS = (
    1.0,
    -1.0 / 6.0,
    1.0 / 120.0,
    -1.0 / 5040.0,
    1.0 / 362880.0,
    -1.0 / 39916800.0,
    1.0 / 6227020800.0,
)


def swapped(value, axis, bit):
    mask = 2**bit
    pairs = [(source, source ^ mask) for source in range(lax.axis_size(axis))]
    return lax.ppermute(value, axis, pairs)


def slot_table(owner_row, box_count, capacity):
    parent_count = owner_row.shape[0]
    onehot = (owner_row[:, None] == jnp.arange(box_count, dtype=jnp.int32)[None, :]).astype(
        jnp.int32
    )
    earlier = jnp.cumsum(onehot, axis=0, dtype=jnp.int32) - onehot
    slot_of = jnp.sum(earlier * onehot, axis=1, dtype=jnp.int32)
    matches = (onehot.T[:, None, :] == 1) & (
        slot_of[None, None, :] == jnp.arange(capacity, dtype=jnp.int32)[None, :, None]
    )
    slot_parent = jnp.sum(
        jnp.where(matches, jnp.arange(parent_count, dtype=jnp.int32)[None, None, :], 0), axis=2
    )
    slot_used = jnp.any(matches, axis=2)
    return (slot_parent, slot_used)


def pick_slot(values, position):
    return lax.dynamic_index_in_dim(values, position, 2, keepdims=False)


def cos_kernel(targets, points):
    shift = 32 - PHASE_BITS
    phase = lax.shift_right_arithmetic(
        lax.shift_left(targets * points, jnp.int32(shift)), jnp.int32(shift)
    )
    offset = NPTS // 4 - jnp.abs(phase)
    y = offset.astype(jnp.float32) * jnp.float32(2.0 * math.pi / NPTS)
    square = y * y
    total = jnp.float32(SIN_TERMS[-1])
    for term in SIN_TERMS[-2::-1]:
        total = total * square + jnp.float32(term)
    return total * y


def split(value):
    high = value.astype(jnp.bfloat16)
    low = (value - high.astype(jnp.float32)).astype(jnp.bfloat16)
    return high, low


def product(left, right):
    rows = left.shape[0]
    left_high, left_low = split(left)
    right_high, right_low = split(right)
    both = jnp.dot(
        jnp.concatenate([left_high, left_low], axis=0),
        right_high,
        preferred_element_type=jnp.float32,
    )
    rest = jnp.dot(left_high, right_low, preferred_element_type=jnp.float32)
    return both[:rows] + both[rows:] + rest


def live(weights, rank):
    rows = lax.broadcasted_iota(jnp.int32, weights.shape, 0)
    return jnp.where(rows < rank, weights, 0.0)


def column(tile, row, begin, length):
    return jnp.transpose(tile)[begin : begin + length, row : row + 1]


def pair_weights(matrix, left, right, left_rank, right_rank):
    width = left.shape[1]
    both = product(matrix, jnp.concatenate([left, right], axis=1))
    return live(both[:, :width], left_rank), live(both[:, width:], right_rank)


def first_kernel(chunk, ranks, points, matrix, mine, arrived, merged):
    step = pl.program_id(0)
    parents, boxes, rank_width = mine.shape[0], mine.shape[1], mine.shape[2]
    for parent in range(parents):
        row = (chunk * pl.num_programs(0) + step) * parents + parent
        tile = points[parent]
        targets = column(tile, TARGETS_LOW, 0, rank_width)
        kernels = [cos_kernel(targets, tile[box : box + 1]) for box in range(boxes)]
        weights = pair_weights(matrix[...], *kernels, ranks[row * boxes], ranks[row * boxes + 1])
        for box in range(boxes):
            stacked = jnp.concatenate([mine[parent, box], arrived[parent, box]], axis=0)
            merged[parent, box] = product(weights[box], stacked)


def later_kernel(chunk, ranks_second, ranks_third, place, points, matrices, mine, arrived, *pool):
    merged = pool[-1]
    step = pl.program_id(0)
    parents, boxes, rank_width = mine.shape[0], mine.shape[1], mine.shape[2]
    for parent in range(parents):
        row = (chunk * pl.num_programs(0) + step) * parents + parent
        tile = points[parent]
        targets = column(tile, TARGETS_LOW, rank_width, rank_width)
        kernels = [
            cos_kernel(targets, tile[POINTS_SECOND + box : POINTS_SECOND + box + 1])
            for box in range(boxes)
        ]
        weights = pair_weights(
            matrices[0], *kernels, ranks_second[row * boxes], ranks_second[row * boxes + 1]
        )
        seconds = []
        for box in range(boxes):
            stacked = jnp.concatenate([mine[parent, box], arrived[parent, box]], axis=0)
            seconds.append(product(weights[box], stacked))
        targets = column(tile, TARGETS_HIGH, 0, 2 * rank_width)
        kernel = cos_kernel(targets, tile[POINTS_THIRD : POINTS_THIRD + 1])
        weights = pair_weights(
            matrices[1],
            kernel[:rank_width],
            kernel[rank_width:],
            ranks_third[row * 2],
            ranks_third[row * 2 + 1],
        )
        third = product(jnp.concatenate(weights, axis=0), jnp.concatenate(seconds, axis=0))
        for child in range(2):
            merged[parent, child] = third[child * rank_width : (child + 1) * rank_width]


def chunk_spec(shape, chunk, steps, per_step):
    block = (per_step,) + tuple(shape[1:])
    rest = (0,) * (len(shape) - 1)
    return pl.BlockSpec(block, lambda step, *_: (chunk * steps + step,) + rest)


def whole_spec(shape):
    rest = (0,) * len(shape)
    return pl.BlockSpec(tuple(shape), lambda step, *_: rest)


def first_level(chunk, ranks, points, matrix, mine, arrived):
    per_step = PER_STEP
    steps = mine.shape[0] // per_step
    return pl.pallas_call(
        functools.partial(first_kernel, chunk),
        grid_spec=pltpu.PrefetchScalarGridSpec(
            num_scalar_prefetch=1,
            grid=(steps,),
            in_specs=[
                chunk_spec(points.shape, chunk, steps, per_step),
                whole_spec(matrix.shape),
                chunk_spec(mine.shape, 0, steps, per_step),
                chunk_spec(arrived.shape, 0, steps, per_step),
            ],
            out_specs=chunk_spec(arrived.shape, 0, steps, per_step),
        ),
        out_shape=jax.ShapeDtypeStruct(arrived.shape, jnp.float32),
        compiler_params=pltpu.CompilerParams(vmem_limit_bytes=VMEM_BYTES),
        name="first_level",
    )(ranks, points, matrix, mine, arrived)


def later_levels(chunk, ranks, place, points, matrices, mine, arrived, pool_shape, pool):
    per_step = PER_STEP
    steps = mine.shape[0] // per_step
    parents = points.shape[0]

    def pool_block(step, ranks_second, ranks_third, place):
        return (place[0] * (parents // per_step) + chunk * steps + step, 0, 0, 0)

    return pl.pallas_call(
        functools.partial(later_kernel, chunk),
        grid_spec=pltpu.PrefetchScalarGridSpec(
            num_scalar_prefetch=3,
            grid=(steps,),
            in_specs=[
                chunk_spec(points.shape, chunk, steps, per_step),
                whole_spec(matrices.shape),
                chunk_spec(mine.shape, 0, steps, per_step),
                chunk_spec(arrived.shape, 0, steps, per_step),
            ]
            + [pl.BlockSpec(memory_space=pl.ANY)] * len(pool),
            out_specs=pl.BlockSpec((per_step,) + pool_shape[1:], pool_block),
        ),
        out_shape=jax.ShapeDtypeStruct(pool_shape, jnp.float32),
        input_output_aliases={7: 0} if pool else {},
        compiler_params=pltpu.CompilerParams(vmem_limit_bytes=VMEM_BYTES),
        name="later_levels",
    )(ranks[0], ranks[1], place, points, matrices, mine, arrived, *pool)


def plan_kernel(chips, limit, chunks, owners, table, counts, slots, rounds, own, ahead, used):
    parents = owners.shape[0]
    count = parents // chunks
    rows = chips + 1
    span = limit * LANES

    def clear(index, carry):
        counts[index] = 0
        return carry

    lax.fori_loop(0, 2 * rows * limit, clear, 0)
    for box in range(2 * chips):
        used[box] = 0

    def take_slot(parent, carry):
        owner = owners[parent]
        slot = used[owner]
        slots[parent] = (owner << SLOT_SHIFT) | slot
        used[owner] = slot + 1
        return carry

    lax.fori_loop(0, parents, take_slot, 0)
    width = chips * parents
    pairs = [(chip, goal) for chip in range(1, chips) for goal in range(chip + 1, chips)]
    last = []
    for direction in range(2):

        def true_chip(chip):
            return chip if direction == 0 else chips - 1 - chip

        total = 0
        for box in range(2 * chips):
            hops = true_chip(box // 2)
            total = total + used[box] * (hops * (hops + 1) // 2)

        def one_round(state):
            step, left, ready, own_head, head, tail, older = state
            ready, own_head, head, tail = list(ready), list(own_head), list(head), list(tail)
            for index in range(count):
                parent = jnp.minimum(step * count + index, parents - 1)
                goal = owners[parent] >> 1
                goal = goal if direction == 0 else chips - 1 - goal
                for chip in range(1, chips):
                    own[chip * parents + jnp.minimum(ready[chip], parents - 1)] = parent
                    here = (goal == chip) & (step < chunks)
                    ready[chip] = ready[chip] + here.astype(jnp.int32)
            seen = older[0]
            for chip in range(chips - 1):
                row = (direction * rows + 1 + chip) * limit + step
                sent = jnp.int32(0)
                for goal in range(chips - 1, chip, -1):
                    onward = pairs.index((chip + 1, goal)) if (chip + 1, goal) in pairs else None
                    for forwarded in (True, False):
                        if forwarded and (chip, goal) not in pairs:
                            continue
                        if forwarded:
                            queue = pairs.index((chip, goal))
                            start, stop = head[queue], seen[queue]
                        else:
                            queue = chip * chips + goal
                            start, stop = own_head[queue], ready[goal]
                        number = jnp.minimum(stop - start, LANES - sent)

                        def move(index, carry):
                            if forwarded:
                                code = ahead[queue * width + start + index]
                            else:
                                code = own[goal * parents + start + index]
                                code = code | (true_chip(chip) << CODE_SHIFT)
                            table[row * LANES + sent + index] = code
                            if onward is not None:
                                ahead[onward * width + tail[onward] + index] = code
                            return carry

                        lax.fori_loop(0, number, move, 0)
                        sent = sent + number
                        if onward is not None:
                            tail[onward] = tail[onward] + number
                        if forwarded:
                            head[queue] = start + number
                        else:
                            own_head[queue] = start + number
                counts[row] = sent
                left = left - sent
            return (
                step + 1,
                left,
                tuple(ready),
                tuple(own_head),
                tuple(head),
                tuple(tail),
                tuple(older[1:]) + (tuple(tail),),
            )

        zero = jnp.int32(0)
        none = (zero,) * len(pairs)
        state = lax.while_loop(
            lambda state: (state[1] > 0) & (state[0] < limit),
            one_round,
            (zero, jnp.int32(total), (zero,) * chips, (zero,) * (chips * chips), none, none, (none,) * LAG),
        )
        last.append(state[0])
    rounds[0] = jnp.maximum(last[0], last[1])


def plan_switch(owner_row, chips):
    parents = owner_row.shape[0]
    limit = round_limit(parents)
    smem = pl.BlockSpec(memory_space=pltpu.SMEM)
    return pl.pallas_call(
        functools.partial(plan_kernel, chips, limit, CHUNKS),
        in_specs=[smem],
        out_specs=[smem] * 4,
        out_shape=[
            jax.ShapeDtypeStruct((2 * (chips + 1) * limit * LANES,), jnp.int32),
            jax.ShapeDtypeStruct((2 * (chips + 1) * limit,), jnp.int32),
            jax.ShapeDtypeStruct((parents,), jnp.int32),
            jax.ShapeDtypeStruct((1,), jnp.int32),
        ],
        scratch_shapes=[
            pltpu.SMEM((chips * parents,), jnp.int32),
            pltpu.SMEM((chips * chips * chips * parents,), jnp.int32),
            pltpu.SMEM((2 * chips,), jnp.int32),
        ],
        name="plan_switch",
    )(owner_row)


def round_limit(parents):
    return 5 * parents // LANES


def round_kernel(chips, limit, parents, receives, fresh, sends, table, counts, slots, place, now, *refs):
    received = refs[: 2 * receives]
    refs = refs[2 * receives + 3 :]
    pool, out, stage = refs[:3]
    outgoing = refs[3 : 3 + 2 * sends]
    kept, sems = refs[-2:]
    z, core = place[0], place[1]
    spots = (z, chips - 1 - z)

    def home(sem, from_chip, parent, source, begin):
        spot = slots[parent]
        owner, slot = spot >> SLOT_SHIFT, spot & ((1 << SLOT_SHIFT) - 1)
        here = (owner >> 1) == z
        same = (owner & 1) == core

        @pl.when(here & same)
        def _():
            copy = pltpu.make_async_copy(source, out.at[:, slot, from_chip, core], sem)
            copy.start() if begin else copy.wait()

        @pl.when(here & jnp.logical_not(same))
        def _():
            copy = pltpu.make_async_copy(source, stage.at[:, slot, from_chip], sem)
            copy.start() if begin else copy.wait()

        return here

    def of_code(code):
        from_chip, parent = code >> CODE_SHIFT, code & ((1 << CODE_SHIFT) - 1)
        return from_chip, parent, from_chip * parents + parent

    def take_in(begin):
        for back in range(receives):
            for direction in range(2):
                step = now[0] - LAG + back
                row = (direction * (chips + 1) + spots[direction]) * limit + jnp.maximum(step, 0)
                number = jnp.where(step >= 0, counts[row], 0)
                base = (2 * back + direction) * LANES

                def one(lane, carry):
                    from_chip, parent, held = of_code(table[row * LANES + lane])
                    source = received[2 * back + direction].at[lane]
                    sem = sems.at[base + lane]
                    here = home(sem, from_chip, parent, source, begin)

                    @pl.when(jnp.logical_not(here))
                    def _():
                        copy = pltpu.make_async_copy(source, pool.at[held], sem)
                        copy.start() if begin else copy.wait()

                    return carry

                lax.fori_loop(0, number, one, 0)

    def send(begin):
        for direction in range(2):
            row = (direction * (chips + 1) + 1 + spots[direction]) * limit + now[0]

            def one(lane, carry):
                _, _, held = of_code(table[row * LANES + lane])
                copy = pltpu.make_async_copy(
                    pool.at[held], outgoing[direction].at[lane], sems.at[direction * LANES + lane]
                )
                copy.start() if begin else copy.wait()
                return carry

            lax.fori_loop(0, counts[row], one, 0)

    def keep(begin):
        def one(member, carry):
            parent = now[0] * fresh + member
            home(sems.at[2 * LANES * max(receives, 1) + member], z, parent, kept.at[member], begin)
            return carry

        lax.fori_loop(0, fresh, one, 0)

    if fresh:
        load = pltpu.make_async_copy(
            pool.at[pl.ds(z * parents + now[0] * fresh, fresh)], kept, sems.at[2 * LANES * max(receives, 1) + fresh]
        )
        load.start()
    take_in(True)
    if fresh:
        load.wait()
        keep(True)
    take_in(False)
    if sends:
        send(True)
    if fresh:
        keep(False)
    if sends:
        send(False)


def switch_round(plan, place, now, received, state, fresh, sends):
    table, counts, slots = plan
    pool, out, stage = state
    parents = slots.shape[0]
    chips = out.shape[2]
    receives = len(received)
    flat = [array for pair in received for array in pair]
    anywhere = pl.BlockSpec(memory_space=pl.ANY)
    inside = pl.BlockSpec(memory_space=pltpu.VMEM)
    lane_shape = jax.ShapeDtypeStruct((LANES,) + pool.shape[1:], jnp.float32)
    first = 5 + len(flat)
    results = pl.pallas_call(
        functools.partial(
            round_kernel, chips, round_limit(parents), parents, receives, fresh, int(sends)
        ),
        grid_spec=pltpu.PrefetchScalarGridSpec(
            num_scalar_prefetch=5,
            grid=(),
            in_specs=[inside] * len(flat) + [anywhere] * 3,
            out_specs=[anywhere] * 3 + [inside] * (2 * int(sends)),
            scratch_shapes=[
                pltpu.VMEM((max(fresh, 1),) + pool.shape[1:], jnp.float32),
                pltpu.SemaphoreType.DMA((2 * LANES * max(receives, 1) + fresh + 1,)),
            ],
        ),
        out_shape=[jax.ShapeDtypeStruct(array.shape, array.dtype) for array in state]
        + [lane_shape] * (2 * int(sends)),
        input_output_aliases={first: 0, first + 1: 1, first + 2: 2},
        compiler_params=pltpu.CompilerParams(vmem_limit_bytes=VMEM_BYTES),
        name="switch_round",
    )(table, counts, slots, place, now, *flat, *state)
    return tuple(results[:3]), tuple(results[3:])


def join_kernel(place, arrived, out_before, out):
    for child in range(2):
        for chip in range(arrived.shape[2]):
            out[child, 0, chip, 0] = arrived[child, 0, chip]


def join_cores(place, arrived, out):
    children, capacity, chips, _, rank_width, width = out.shape
    return pl.pallas_call(
        join_kernel,
        grid_spec=pltpu.PrefetchScalarGridSpec(
            num_scalar_prefetch=1,
            grid=(capacity,),
            in_specs=[
                pl.BlockSpec(
                    (children, 1, chips, rank_width, width), lambda slot, place: (0, slot, 0, 0, 0)
                ),
                pl.BlockSpec(memory_space=pl.ANY),
            ],
            out_specs=pl.BlockSpec(
                (children, 1, chips, 1, rank_width, width),
                lambda slot, place: (0, slot, 0, 1 - place[1], 0, 0),
            ),
        ),
        out_shape=jax.ShapeDtypeStruct(out.shape, out.dtype),
        input_output_aliases={2: 0},
        compiler_params=pltpu.CompilerParams(vmem_limit_bytes=VMEM_BYTES),
        name="join_cores",
    )(place, arrived, out)


def along_line(value, chips, up):
    pairs = []
    for chip in range(chips - 1):
        for core in range(2):
            low, high = 2 * chip + core, 2 * (chip + 1) + core
            pairs.append((low, high) if up else (high, low))
    return lax.ppermute(value, "box", pairs)


def per_device(
    coeffs,
    skeleton_first,
    skeleton_second,
    skeleton_third,
    checks_first,
    checks_second,
    checks_third,
    ranks_first,
    ranks_second,
    ranks_third,
    interpolants,
    owners,
):
    tbit_index = lax.axis_index("tbit")
    box_index = lax.axis_index("box")
    box_count = lax.axis_size("box")
    parent_count = coeffs.shape[0]
    rank_width = coeffs.shape[3]
    capacity = 2 * parent_count // box_count
    group_count = 2 * box_count
    local_boxes = 2 * box_index + jnp.arange(2, dtype=jnp.int32)[None, :, None]

    def targets_of(checks, per_parent, picked, width):
        boxes = per_parent * parent_count
        absolute = jnp.arange(boxes, dtype=jnp.int32)[:, None] * (NPTS // boxes) + checks
        return lax.dynamic_index_in_dim(absolute.reshape(parent_count, -1, width), picked, 1)

    def first_points(slot):
        box = 4 * local_boxes + 2 * (slot % 2) + slot // 2
        return box * (NPTS // (4 * group_count)) + pick_slot(skeleton_first, slot)

    def second_points(slot):
        box = 2 * local_boxes + slot % 2
        return box * (NPTS // (2 * group_count)) + pick_slot(skeleton_second, slot)

    partner_high = jnp.bitwise_xor(tbit_index, 2)
    partner_low = jnp.bitwise_xor(tbit_index, 1)
    points_third = local_boxes * (NPTS // group_count) + pick_slot(skeleton_third, tbit_index)
    low_targets = jnp.concatenate(
        [
            targets_of(checks_first, 2, tbit_index // 2, rank_width),
            targets_of(checks_second, 4, tbit_index, rank_width),
        ],
        axis=2,
    )
    high_targets = targets_of(checks_third, 8, tbit_index, 2 * rank_width)
    points = jnp.concatenate(
        [
            jnp.concatenate([first_points(tbit_index), first_points(partner_high)], axis=2),
            jnp.concatenate([second_points(tbit_index), second_points(partner_low)], axis=2),
            points_third.reshape(parent_count, 1, 2 * rank_width),
            low_targets,
            high_targets,
            jnp.zeros_like(high_targets),
        ],
        axis=1,
    )
    rank_one = ranks_first.reshape(-1)
    rank_two = ranks_second.reshape(-1)
    rank_three = lax.dynamic_index_in_dim(
        lax.dynamic_index_in_dim(ranks_third, tbit_index, 1, keepdims=False),
        box_index,
        2,
        keepdims=False,
    ).reshape(-1)

    mine = coeffs[:, :, 0]
    count = parent_count // CHUNKS
    chips = box_count // 2
    networked = chips <= 4
    place = jnp.stack([box_index // 2, box_index % 2]).astype(jnp.int32)
    owner_row = lax.dynamic_index_in_dim(owners, tbit_index, 0, keepdims=False)
    width = coeffs.shape[-1]
    pool_shape = (chips * parent_count, 2, rank_width, width)
    if not networked:
        place = jnp.zeros_like(place)
        pool_shape = (parent_count, 2, rank_width, width)

    parts, arrived = [], []
    for chunk in range(CHUNKS):
        source = mine
        if chunk > 0:
            source, _ = lax.optimization_barrier((mine, arrived[-1]))
        parts.append(source[chunk * count : (chunk + 1) * count])
        arrived.append(swapped(parts[-1], "tbit", 1))

    if networked:
        *plan, rounds = plan_switch(owner_row, chips)
        out = jnp.zeros((2, capacity, chips, 2, rank_width, width), jnp.float32)
        stage = jnp.zeros((2, capacity, chips, rank_width, width), jnp.float32)
        arrived[0], points, plan, rounds, out, stage = lax.optimization_barrier(
            (arrived[0], points, plan, rounds, out, stage)
        )
        most = jnp.broadcast_to(rounds, (8, 128))
        most = jnp.maximum(most, swapped(most, "tbit", 1))
        most = jnp.maximum(most, swapped(most, "tbit", 0))
        most = jnp.maximum(most[0, 0], STATIC_ROUNDS)
        arrived[2], most = lax.optimization_barrier((arrived[2], most))

    second_arrived = []

    def levels(chunk, pool):
        first = first_level(chunk, rank_one, points, interpolants[0], parts[chunk], arrived[chunk])
        outgoing = first
        if chunk > 0:
            outgoing, _ = lax.optimization_barrier((outgoing, second_arrived[-1]))
        second_arrived.append(swapped(outgoing, "tbit", 0))
        return later_levels(
            chunk,
            (rank_two, rank_three),
            place,
            points,
            interpolants[1:],
            first,
            second_arrived[chunk],
            pool_shape,
            pool,
        )

    if not networked:
        pool = levels(0, ())
        for chunk in range(1, CHUNKS):
            pool = levels(chunk, (pool,))
        slot_parent, slot_used = slot_table(owner_row, box_count, capacity)
        outgoing = jnp.take(jnp.swapaxes(pool, 0, 1), slot_parent.T, axis=1)
        outgoing = jnp.where(slot_used.T[None, :, :, None, None], outgoing, 0.0)
        switched = lax.all_to_all(outgoing, "box", split_axis=2, concat_axis=2, tiled=True)
        return switched[None, None]

    state = (None, out, stage)
    received = []

    def exchange(packed):
        return (along_line(packed[0], chips, True), along_line(packed[1], chips, False))

    for step in range(STATIC_ROUNDS):
        fresh = 0
        if step < CHUNKS:
            state = (levels(step, state[:1] if step else ()),) + state[1:]
            fresh = count
        now = jnp.full((1,), step, jnp.int32)
        oldest = received[step - LAG : step - LAG + 1] if step >= LAG else []
        state, packed = switch_round(plan, place, now, oldest, state, fresh, True)
        received.append(exchange(packed))

    def more(carry):
        return carry[0] < most

    def again(carry):
        step, state, waiting = carry
        state, packed = switch_round(plan, place, step[None], waiting[:1], state, 0, True)
        return (step + 1, state, waiting[1:] + (exchange(packed),))

    step, state, waiting = lax.while_loop(
        more, again, (jnp.int32(STATIC_ROUNDS), state, tuple(received[-LAG:]))
    )
    state, _ = switch_round(plan, place, step[None], waiting, state, 0, False)
    _, out, stage = state
    crossed = lax.ppermute(stage, "box", [(box, box ^ 1) for box in range(box_count)])
    out = join_cores(place, crossed, out)
    return out.reshape(1, 1, 2, capacity, box_count, rank_width, width)


def solution(mesh):
    return jax.shard_map(
        per_device,
        mesh=mesh,
        in_specs=(
            P(None, "box", "tbit", None, None),
            P(None, "box", None, None),
            P(None, "box", None, None),
            P(None, "box", None, None),
            P(),
            P(),
            P(),
            P(None, "box", "tbit"),
            P(None, "box", "tbit"),
            P(),
            P(),
            P(),
        ),
        out_specs=P("tbit", "box", None, None, None, None, None),
        check_vma=False,
    )
```

time: 1730 us -> 451 us (0.26)
  Pallas kernels: 855 us -> 128 us
  starting transfers between devices: 637 us -> 100 us
  local copies, waits for them, and re-layouts: 102 us -> 36.8 us
  waiting for transfers between devices: 116 us -> 177 us
    ppermute x24, starting transfers between devices: 600 us -> 77 us  [along_line(): return lax.ppermute(value, 'box', pairs)]
    pallas_call x14, Pallas kernels: 502 us -> 53.2 us  [the longest x13 43.1 us: switch_round(): pl.pallas_call(functools.partial(round_kernel, chips, round_limit(parents...]
    pallas_call x1, Pallas kernels: 256 us -> 7.69 us  [join_cores(): pl.pallas_call(join_kernel, grid_spec=pltpu.PrefetchScalarGridSpec(num_sc...]
    ppermute x24, waiting for transfers between devices: 37.5 us -> 104 us  [along_line(): return lax.ppermute(value, 'box', pairs)]
    unnamed x80 -> x36, local copies, waits for them, and re-layouts: 60.6 us -> 5.65 us
    ppermute x16 -> x18, starting transfers between devices: 36.9 us -> 22.9 us  [swapped(): return lax.ppermute(value, axis, pairs)]
    ppermute x16 -> x18, waiting for transfers between devices: 65.4 us -> 59.4 us  [swapped(): return lax.ppermute(value, axis, pairs)]
  transfers between devices with their start and end apart: 41 -> 43, of which waited for: 12 -> 29; matrix products, arithmetic and copies ran while one was open for 2% -> 8% of each run, Pallas kernels for 33% -> 26%
where the time goes in v3:
time: 451 us; the launch traced here: 449 us
  waiting for transfers between devices  177 us (39%)
  Pallas kernels  128 us (28%)
  starting transfers between devices  100 us (22%)
  local copies, waits for them, and re-layouts  36.8 us (8%)
  other arithmetic  4.57 us (1%)
    ppermute x24, waiting for transfers between devices, along_line(): return lax.ppermute(value, 'box', pairs)  104 us
    ppermute x24, starting transfers between devices, along_line(): return lax.ppermute(value, 'box', pairs)  77 us
    ppermute x18, waiting for transfers between devices, swapped(): return lax.ppermute(value, axis, pairs)  59.4 us
    pallas_call x13, Pallas kernels, switch_round(): pl.pallas_call(functools.partial(round_kernel, chips, round_limit(parents...  43.1 us
    pallas_call x8, Pallas kernels, later_levels(): pl.pallas_call(functools.partial(later_kernel, chunk), grid_spec=pltpu.Pr...  42.3 us
    pallas_call x8, Pallas kernels, first_level(): pl.pallas_call(functools.partial(first_kernel, chunk), grid_spec=pltpu.Pr...  25.1 us
    ppermute x18, starting transfers between devices, swapped(): return lax.ppermute(value, axis, pairs)  22.9 us
    ppermute x1, waiting for transfers between devices, per_device(): lax.ppermute(stage, 'box', [(box, box ^ 1) for box in range(box_count)])  13.4 us
  transfers between devices with their start and end apart: 43, of which 29 were waited for; matrix products, arithmetic and copies ran while one was open for 8% of the time, Pallas kernels for 26%

profile of v3, /device:TPU:0, one launch (start us, length us, event | category | flops | bytes accessed | tf_op | source)
XLA Modules:
  0.0 448.6 jit_solution(4606926888868834341)
XLA Ops:
  11.9 10.1 %plan_switch.1 = (s32[3200]{0:T(1024)}, s32[400]{0:T(512)S(1)}, s32[64]{0:T(128)S(1)}, s32[1]{0:T(128)}) custom-call(s32[64]{0:T(128)} %fusion.owners), custom_call_target="tpu_custom_call" | custom-call | tf_op jit(solution)/shard_map/plan_switch/pallas_call | solution.py:330
  35.2 18.1 %collective-permute-done.3.arrived = f32[8,2,64,256]{3,2,1,0:T(8,128)S(1)} collective-permute-done((f32[8,2,64,256]{3,2,1,0:T(8,128)S(1)}, f32[8,2,64,256]{3,2,1,0:T(8,128)S(1)}, u32[]{:S(2)}, u32[]{:S(2)}) %collective-permute-start.3) | collective-permute-done | bytes 1048608 | tf_op jit(solution)/shard_map/ppermute | solution.py:40
  61.8 16.4 %collective-permute-done.10 = s32[8,128]{1,0:T(8,128)S(1)} collective-permute-done((s32[8,128]{1,0:T(8,128)S(1)}, s32[8,128]{1,0:T(8,128)S(1)}, u32[]{:S(2)}, u32[]{:S(2)}) %collective-permute-start.10) | collective-permute-done | bytes 4128 | tf_op jit(solution)/shard_map/ppermute | solution.py:40
  91.3 16.1 %collective-permute-done.9.arrived = f32[8,2,64,256]{3,2,1,0:T(8,128)S(1)} collective-permute-done((f32[8,2,64,256]{3,2,1,0:T(8,128)S(1)}, f32[8,2,64,256]{3,2,1,0:T(8,128)S(1)}, u32[]{:S(2)}, u32[]{:S(2)}) %collective-permute-start.9) | collective-permute-done | bytes 1048608 | tf_op jit(solution)/shard_map/ppermute | solution.py:40
  139.6 8.3 %broadcast_in_dim.25.refs_1_ = f32[2,16,4,2,64,256]{5,4,3,2,1,0:T(8,128)} broadcast(f32[]{:T(128)} %constant.153.clone.1), dimensions={} | broadcast | bytes 16777220 | tf_op jit(solution)/shard_map/broadcast_in_dim | solution.py:610
  194.3 6.2 %later_levels.11.refs_2_ = f32[256,2,64,256]{3,2,1,0:T(8,128)} custom-call(s32[128]{0:T(128)S(1)} %reshape.114.ranks_second, s32[128]{0:T(128)S(1)} %reshape.115.ranks_third, s32[2]{0:T(128)S(1)} %pad_add_fusion.3.place, s32[64,8,128]{2,1,0:T(8,128)S(1)} %concatenate.15.points, f32[2,64,64]{2,1,0:T(8,128)S(1)} %slice.52.matrices, ...), custom_call_target="tpu_custom_call", output_to_operand_aliasing={{}: (7, {})} | custom-call | tf_op jit(solution)/shard_map/later_levels/pallas_call | solution.py:200
  207.1 5.6 %collective-permute-start.16 = (f32[8,2,64,256]{3,2,1,0:T(8,128)S(1)}, f32[8,2,64,256]{3,2,1,0:T(8,128)S(1)}, u32[]{:S(2)}, u32[]{:S(2)}) collective-permute-start(f32[8,2,64,256]{3,2,1,0:T(8,128)S(1)} %get-tuple-element.207), channel_id=1, source_target_pairs={{0,2},{1,3},{2,4},{3,5},{4,6},{5,7},{8,10},{9,11},{10,12},{11,13},... | collective-permute-start | bytes 3145736 | tf_op jit(solution)/shard_map/ppermute | solution.py:518
  269.5 6.0 %collective-permute-done.31.refs_1_ = f32[8,2,64,256]{3,2,1,0:T(8,128)S(1)} collective-permute-done((f32[8,2,64,256]{3,2,1,0:T(8,128)S(1)}, f32[8,2,64,256]{3,2,1,0:T(8,128)S(1)}, u32[]{:S(2)}, u32[]{:S(2)}) %collective-permute-start.31) | collective-permute-done | bytes 1048608 | tf_op jit(solution)/shard_map/ppermute | solution.py:518
  292.0 6.0 %collective-permute-done.25.refs_1_ = f32[8,2,64,256]{3,2,1,0:T(8,128)S(1)} collective-permute-done((f32[8,2,64,256]{3,2,1,0:T(8,128)S(1)}, f32[8,2,64,256]{3,2,1,0:T(8,128)S(1)}, u32[]{:S(2)}, u32[]{:S(2)}) %collective-permute-start.25) | collective-permute-done | bytes 1048608 | tf_op jit(solution)/shard_map/ppermute | solution.py:518
  308.0 6.4 %collective-permute-done.34.refs_0_ = f32[8,2,64,256]{3,2,1,0:T(8,128)S(1)} collective-permute-done((f32[8,2,64,256]{3,2,1,0:T(8,128)S(1)}, f32[8,2,64,256]{3,2,1,0:T(8,128)S(1)}, u32[]{:S(2)}, u32[]{:S(2)}) %collective-permute-start.34) | collective-permute-done | bytes 1048608 | tf_op jit(solution)/shard_map/ppermute | solution.py:518
  314.4 6.0 %collective-permute-done.35.refs_1_ = f32[8,2,64,256]{3,2,1,0:T(8,128)S(1)} collective-permute-done((f32[8,2,64,256]{3,2,1,0:T(8,128)S(1)}, f32[8,2,64,256]{3,2,1,0:T(8,128)S(1)}, u32[]{:S(2)}, u32[]{:S(2)}) %collective-permute-start.35) | collective-permute-done | bytes 1048608 | tf_op jit(solution)/shard_map/ppermute | solution.py:518
  329.4 7.6 %collective-permute-done.32.refs_0_ = f32[8,2,64,256]{3,2,1,0:T(8,128)S(1)} collective-permute-done((f32[8,2,64,256]{3,2,1,0:T(8,128)S(1)}, f32[8,2,64,256]{3,2,1,0:T(8,128)S(1)}, u32[]{:S(2)}, u32[]{:S(2)}) %collective-permute-start.32) | collective-permute-done | bytes 1048608 | tf_op jit(solution)/shard_map/ppermute | solution.py:518
  336.9 6.0 %collective-permute-done.33.refs_1_ = f32[8,2,64,256]{3,2,1,0:T(8,128)S(1)} collective-permute-done((f32[8,2,64,256]{3,2,1,0:T(8,128)S(1)}, f32[8,2,64,256]{3,2,1,0:T(8,128)S(1)}, u32[]{:S(2)}, u32[]{:S(2)}) %collective-permute-start.33) | collective-permute-done | bytes 1048608 | tf_op jit(solution)/shard_map/ppermute | solution.py:518
  351.8 7.5 %collective-permute-done.38.refs_0_ = f32[8,2,64,256]{3,2,1,0:T(8,128)S(1)} collective-permute-done((f32[8,2,64,256]{3,2,1,0:T(8,128)S(1)}, f32[8,2,64,256]{3,2,1,0:T(8,128)S(1)}, u32[]{:S(2)}, u32[]{:S(2)}) %collective-permute-start.38) | collective-permute-done | bytes 1048608 | tf_op jit(solution)/shard_map/ppermute | solution.py:518
  359.4 6.0 %collective-permute-done.39.refs_1_ = f32[8,2,64,256]{3,2,1,0:T(8,128)S(1)} collective-permute-done((f32[8,2,64,256]{3,2,1,0:T(8,128)S(1)}, f32[8,2,64,256]{3,2,1,0:T(8,128)S(1)}, u32[]{:S(2)}, u32[]{:S(2)}) %collective-permute-start.39) | collective-permute-done | bytes 1048608 | tf_op jit(solution)/shard_map/ppermute | solution.py:518
  367.4 5.9 %collective-permute-start.40 = (f32[8,2,64,256]{3,2,1,0:T(8,128)S(1)}, f32[8,2,64,256]{3,2,1,0:T(8,128)}, u32[]{:S(2)}, u32[]{:S(2)}) collective-permute-start(f32[8,2,64,256]{3,2,1,0:T(8,128)S(1)} %get-tuple-element.258), channel_id=1, source_target_pairs={{0,2},{1,3},{2,4},{3,5},{4,6},{5,7},{8,10},{9,11},{10,12},{11,13},... | collective-permute-start | bytes 3145736 | tf_op jit(solution)/shard_map/ppermute | solution.py:518
  374.6 7.2 %collective-permute-done.36.refs_0_ = f32[8,2,64,256]{3,2,1,0:T(8,128)S(1)} collective-permute-done((f32[8,2,64,256]{3,2,1,0:T(8,128)S(1)}, f32[8,2,64,256]{3,2,1,0:T(8,128)S(1)}, u32[]{:S(2)}, u32[]{:S(2)}) %collective-permute-start.36) | collective-permute-done | bytes 1048608 | tf_op jit(solution)/shard_map/ppermute | solution.py:518
  381.8 6.0 %collective-permute-done.37.refs_1_ = f32[8,2,64,256]{3,2,1,0:T(8,128)S(1)} collective-permute-done((f32[8,2,64,256]{3,2,1,0:T(8,128)S(1)}, f32[8,2,64,256]{3,2,1,0:T(8,128)S(1)}, u32[]{:S(2)}, u32[]{:S(2)}) %collective-permute-start.37) | collective-permute-done | bytes 1048608 | tf_op jit(solution)/shard_map/ppermute | solution.py:518
  390.9 6.4 %collective-permute-start.42 = (f32[8,2,64,256]{3,2,1,0:T(8,128)}, f32[8,2,64,256]{3,2,1,0:T(8,128)}, u32[]{:S(2)}, u32[]{:S(2)}) collective-permute-start(f32[8,2,64,256]{3,2,1,0:T(8,128)} %get-tuple-element.260), channel_id=1, source_target_pairs={{0,2},{1,3},{2,4},{3,5},{4,6},{5,7},{8,10},{9,11},{10,12},{11,13},... | collective-permute-start | bytes 3145736 | tf_op jit(solution)/shard_map/ppermute | solution.py:518
  398.6 5.7 %collective-permute-done.40 = f32[8,2,64,256]{3,2,1,0:T(8,128)} collective-permute-done((f32[8,2,64,256]{3,2,1,0:T(8,128)S(1)}, f32[8,2,64,256]{3,2,1,0:T(8,128)}, u32[]{:S(2)}, u32[]{:S(2)}) %collective-permute-start.40) | collective-permute-done | bytes 1048608 | tf_op jit(solution)/shard_map/ppermute | solution.py:518
  404.3 6.1 %collective-permute-done.41 = f32[8,2,64,256]{3,2,1,0:T(8,128)} collective-permute-done((f32[8,2,64,256]{3,2,1,0:T(8,128)S(1)}, f32[8,2,64,256]{3,2,1,0:T(8,128)}, u32[]{:S(2)}, u32[]{:S(2)}) %collective-permute-start.41) | collective-permute-done | bytes 1048608 | tf_op jit(solution)/shard_map/ppermute | solution.py:518
  410.4 8.6 %collective-permute-done.42 = f32[8,2,64,256]{3,2,1,0:T(8,128)} collective-permute-done((f32[8,2,64,256]{3,2,1,0:T(8,128)}, f32[8,2,64,256]{3,2,1,0:T(8,128)}, u32[]{:S(2)}, u32[]{:S(2)}) %collective-permute-start.42) | collective-permute-done | bytes 1048608 | tf_op jit(solution)/shard_map/ppermute | solution.py:518
  427.5 13.4 %collective-permute-done.44.arrived = f32[2,16,4,64,256]{4,3,2,1,0:T(8,128)S(1)} collective-permute-done((f32[2,16,4,64,256]{4,3,2,1,0:T(8,128)}, f32[2,16,4,64,256]{4,3,2,1,0:T(8,128)S(1)}, u32[]{:S(2)}, u32[]{:S(2)}) %collective-permute-start.44) | collective-permute-done | bytes 8388640 | tf_op jit(solution)/shard_map/ppermute | solution.py:680
  440.9 7.7 %join_cores.1 = f32[2,16,4,2,64,256]{5,4,3,2,1,0:T(8,128)} custom-call(s32[2]{0:T(128)S(1)} %get-tuple-element.521, f32[2,16,4,64,256]{4,3,2,1,0:T(8,128)S(1)} %collective-permute-done.44.arrived, f32[2,16,4,2,64,256]{5,4,3,2,1,0:T(8,128)} %get-tuple-element.272.out_before), custom_call_target="tpu_custom_call", output_to_operand_aliasing={{}: (2, {})} | custom-call | tf_op jit(solution)/shard_map/join_cores/pallas_call | solution.py:489
  (185 shorter events, 247.9 us)
Async XLA Ops:
  59.1 30.7 %collective-permute-start.5 = (f32[8,2,64,256]{3,2,1,0:T(8,128)S(1)}, f32[8,2,64,256]{3,2,1,0:T(8,128)S(1)}, u32[]{:S(2)}, u32[]{:S(2)}) collective-permute-start(f32[8,2,64,256]{3,2,1,0:T(8,128)S(1)} %first_level.8.mine), channel_id=1, source_target_pairs={{0,8},{8,0},{16,24},{24,16},{1,9},{9,1},{17,25},{25,17},{2,10},{10... | collective-permute-start | bytes 3145736 | tf_op jit(solution)/shard_map/ppermute | solution.py:40
  133.2 37.8 %collective-permute-start.19 = (f32[8,2,64,256]{3,2,1,0:T(8,128)S(1)}, f32[8,2,64,256]{3,2,1,0:T(8,128)S(1)}, u32[]{:S(2)}, u32[]{:S(2)}) collective-permute-start(f32[8,2,64,256]{3,2,1,0:T(8,128)S(1)} %slice.59.mine), channel_id=1, source_target_pairs={{0,16},{8,24},{16,0},{24,8},{1,17},{9,25},{17,1},{25,9},{2,18},{10... | collective-permute-start | bytes 3145736 | tf_op jit(solution)/shard_map/ppermute | solution.py:40
  138.5 36.8 %collective-permute-start.20 = (f32[8,2,64,256]{3,2,1,0:T(8,128)S(1)}, f32[8,2,64,256]{3,2,1,0:T(8,128)S(1)}, u32[]{:S(2)}, u32[]{:S(2)}) collective-permute-start(f32[8,2,64,256]{3,2,1,0:T(8,128)S(1)} %first_level.13.mine), channel_id=1, source_target_pairs={{0,8},{8,0},{16,24},{24,16},{1,9},{9,1},{17,25},{25,17},{2,10},{10... | collective-permute-start | bytes 3145736 | tf_op jit(solution)/shard_map/ppermute | solution.py:40
  166.4 35.6 %collective-permute-start.6 = (f32[8,2,64,256]{3,2,1,0:T(8,128)S(1)}, f32[8,2,64,256]{3,2,1,0:T(8,128)S(1)}, u32[]{:S(2)}, u32[]{:S(2)}) collective-permute-start(f32[8,2,64,256]{3,2,1,0:T(8,128)S(1)} %get-tuple-element.191), channel_id=1, source_target_pairs={{0,2},{1,3},{2,4},{3,5},{4,6},{5,7},{8,10},{9,11},{10,12},{11,13},... | collective-permute-start | bytes 3145736 | tf_op jit(solution)/shard_map/ppermute | solution.py:518
  176.6 36.1 %collective-permute-start.26 = (f32[8,2,64,256]{3,2,1,0:T(8,128)S(1)}, f32[8,2,64,256]{3,2,1,0:T(8,128)S(1)}, u32[]{:S(2)}, u32[]{:S(2)}) collective-permute-start(f32[8,2,64,256]{3,2,1,0:T(8,128)S(1)} %slice.60.mine), channel_id=1, source_target_pairs={{0,16},{8,24},{16,0},{24,8},{1,17},{9,25},{17,1},{25,9},{2,18},{10... | collective-permute-start | bytes 3145736 | tf_op jit(solution)/shard_map/ppermute | solution.py:40
  179.6 37.4 %collective-permute-start.21 = (f32[8,2,64,256]{3,2,1,0:T(8,128)S(1)}, f32[8,2,64,256]{3,2,1,0:T(8,128)S(1)}, u32[]{:S(2)}, u32[]{:S(2)}) collective-permute-start(f32[8,2,64,256]{3,2,1,0:T(8,128)S(1)} %first_level.12.mine), channel_id=1, source_target_pairs={{0,8},{8,0},{16,24},{24,16},{1,9},{9,1},{17,25},{25,17},{2,10},{10... | collective-permute-start | bytes 3145736 | tf_op jit(solution)/shard_map/ppermute | solution.py:40
  188.9 35.6 %collective-permute-start.22 = (f32[8,2,64,256]{3,2,1,0:T(8,128)S(1)}, f32[8,2,64,256]{3,2,1,0:T(8,128)S(1)}, u32[]{:S(2)}, u32[]{:S(2)}) collective-permute-start(f32[8,2,64,256]{3,2,1,0:T(8,128)S(1)} %get-tuple-element.213), channel_id=1, source_target_pairs={{0,2},{1,3},{2,4},{3,5},{4,6},{5,7},{8,10},{9,11},{10,12},{11,13},... | collective-permute-start | bytes 3145736 | tf_op jit(solution)/shard_map/ppermute | solution.py:518
  207.1 39.9 %collective-permute-start.16 = (f32[8,2,64,256]{3,2,1,0:T(8,128)S(1)}, f32[8,2,64,256]{3,2,1,0:T(8,128)S(1)}, u32[]{:S(2)}, u32[]{:S(2)}) collective-permute-start(f32[8,2,64,256]{3,2,1,0:T(8,128)S(1)} %get-tuple-element.207), channel_id=1, source_target_pairs={{0,2},{1,3},{2,4},{3,5},{4,6},{5,7},{8,10},{9,11},{10,12},{11,13},... | collective-permute-start | bytes 3145736 | tf_op jit(solution)/shard_map/ppermute | solution.py:518
  215.7 34.3 %collective-permute-start.17 = (f32[8,2,64,256]{3,2,1,0:T(8,128)S(1)}, f32[8,2,64,256]{3,2,1,0:T(8,128)S(1)}, u32[]{:S(2)}, u32[]{:S(2)}) collective-permute-start(f32[8,2,64,256]{3,2,1,0:T(8,128)S(1)} %get-tuple-element.208), channel_id=1, source_target_pairs={{2,0},{3,1},{4,2},{5,3},{6,4},{7,5},{10,8},{11,9},{12,10},{13,11},... | collective-permute-start | bytes 3145736 | tf_op jit(solution)/shard_map/ppermute | solution.py:518
  218.3 35.4 %collective-permute-start.27 = (f32[8,2,64,256]{3,2,1,0:T(8,128)S(1)}, f32[8,2,64,256]{3,2,1,0:T(8,128)S(1)}, u32[]{:S(2)}, u32[]{:S(2)}) collective-permute-start(f32[8,2,64,256]{3,2,1,0:T(8,128)S(1)} %slice.61.mine), channel_id=1, source_target_pairs={{0,16},{8,24},{16,0},{24,8},{1,17},{9,25},{17,1},{25,9},{2,18},{10... | collective-permute-start | bytes 3145736 | tf_op jit(solution)/shard_map/ppermute | solution.py:40
  224.5 32.2 %collective-permute-start.28 = (f32[8,2,64,256]{3,2,1,0:T(8,128)S(1)}, f32[8,2,64,256]{3,2,1,0:T(8,128)S(1)}, u32[]{:S(2)}, u32[]{:S(2)}) collective-permute-start(f32[8,2,64,256]{3,2,1,0:T(8,128)S(1)} %first_level.15.mine), channel_id=1, source_target_pairs={{0,8},{8,0},{16,24},{24,16},{1,9},{9,1},{17,25},{25,17},{2,10},{10... | collective-permute-start | bytes 3145736 | tf_op jit(solution)/shard_map/ppermute | solution.py:40
  239.4 30.1 %collective-permute-start.30 = (f32[8,2,64,256]{3,2,1,0:T(8,128)S(1)}, f32[8,2,64,256]{3,2,1,0:T(8,128)S(1)}, u32[]{:S(2)}, u32[]{:S(2)}) collective-permute-start(f32[8,2,64,256]{3,2,1,0:T(8,128)S(1)} %get-tuple-element.227), channel_id=1, source_target_pairs={{0,2},{1,3},{2,4},{3,5},{4,6},{5,7},{8,10},{9,11},{10,12},{11,13},... | collective-permute-start | bytes 3145736 | tf_op jit(solution)/shard_map/ppermute | solution.py:518
  257.3 34.6 %collective-permute-start.24 = (f32[8,2,64,256]{3,2,1,0:T(8,128)S(1)}, f32[8,2,64,256]{3,2,1,0:T(8,128)S(1)}, u32[]{:S(2)}, u32[]{:S(2)}) collective-permute-start(f32[8,2,64,256]{3,2,1,0:T(8,128)S(1)} %get-tuple-element.221), channel_id=1, source_target_pairs={{0,2},{1,3},{2,4},{3,5},{4,6},{5,7},{8,10},{9,11},{10,12},{11,13},... | collective-permute-start | bytes 3145736 | tf_op jit(solution)/shard_map/ppermute | solution.py:518
  261.6 36.3 %collective-permute-start.25 = (f32[8,2,64,256]{3,2,1,0:T(8,128)S(1)}, f32[8,2,64,256]{3,2,1,0:T(8,128)S(1)}, u32[]{:S(2)}, u32[]{:S(2)}) collective-permute-start(f32[8,2,64,256]{3,2,1,0:T(8,128)S(1)} %get-tuple-element.222), channel_id=1, source_target_pairs={{2,0},{3,1},{4,2},{5,3},{6,4},{7,5},{10,8},{11,9},{12,10},{13,11},... | collective-permute-start | bytes 3145736 | tf_op jit(solution)/shard_map/ppermute | solution.py:518
  279.3 35.1 %collective-permute-start.34 = (f32[8,2,64,256]{3,2,1,0:T(8,128)S(1)}, f32[8,2,64,256]{3,2,1,0:T(8,128)S(1)}, u32[]{:S(2)}, u32[]{:S(2)}) collective-permute-start(f32[8,2,64,256]{3,2,1,0:T(8,128)S(1)} %get-tuple-element.237), channel_id=1, source_target_pairs={{0,2},{1,3},{2,4},{3,5},{4,6},{5,7},{8,10},{9,11},{10,12},{11,13},... | collective-permute-start | bytes 3145736 | tf_op jit(solution)/shard_map/ppermute | solution.py:518
  283.8 36.6 %collective-permute-start.35 = (f32[8,2,64,256]{3,2,1,0:T(8,128)S(1)}, f32[8,2,64,256]{3,2,1,0:T(8,128)S(1)}, u32[]{:S(2)}, u32[]{:S(2)}) collective-permute-start(f32[8,2,64,256]{3,2,1,0:T(8,128)S(1)} %get-tuple-element.238), channel_id=1, source_target_pairs={{2,0},{3,1},{4,2},{5,3},{6,4},{7,5},{10,8},{11,9},{12,10},{13,11},... | collective-permute-start | bytes 3145736 | tf_op jit(solution)/shard_map/ppermute | solution.py:518
  301.6 35.3 %collective-permute-start.32 = (f32[8,2,64,256]{3,2,1,0:T(8,128)S(1)}, f32[8,2,64,256]{3,2,1,0:T(8,128)S(1)}, u32[]{:S(2)}, u32[]{:S(2)}) collective-permute-start(f32[8,2,64,256]{3,2,1,0:T(8,128)S(1)} %get-tuple-element.235), channel_id=1, source_target_pairs={{0,2},{1,3},{2,4},{3,5},{4,6},{5,7},{8,10},{9,11},{10,12},{11,13},... | collective-permute-start | bytes 3145736 | tf_op jit(solution)/shard_map/ppermute | solution.py:518
  306.7 36.1 %collective-permute-start.33 = (f32[8,2,64,256]{3,2,1,0:T(8,128)S(1)}, f32[8,2,64,256]{3,2,1,0:T(8,128)S(1)}, u32[]{:S(2)}, u32[]{:S(2)}) collective-permute-start(f32[8,2,64,256]{3,2,1,0:T(8,128)S(1)} %get-tuple-element.236), channel_id=1, source_target_pairs={{2,0},{3,1},{4,2},{5,3},{6,4},{7,5},{10,8},{11,9},{12,10},{13,11},... | collective-permute-start | bytes 3145736 | tf_op jit(solution)/shard_map/ppermute | solution.py:518
  322.5 36.9 %collective-permute-start.38 = (f32[8,2,64,256]{3,2,1,0:T(8,128)S(1)}, f32[8,2,64,256]{3,2,1,0:T(8,128)S(1)}, u32[]{:S(2)}, u32[]{:S(2)}) collective-permute-start(f32[8,2,64,256]{3,2,1,0:T(8,128)S(1)} %get-tuple-element.247), channel_id=1, source_target_pairs={{0,2},{1,3},{2,4},{3,5},{4,6},{5,7},{8,10},{9,11},{10,12},{11,13},... | collective-permute-start | bytes 3145736 | tf_op jit(solution)/shard_map/ppermute | solution.py:518
  328.1 37.3 %collective-permute-start.39 = (f32[8,2,64,256]{3,2,1,0:T(8,128)S(1)}, f32[8,2,64,256]{3,2,1,0:T(8,128)S(1)}, u32[]{:S(2)}, u32[]{:S(2)}) collective-permute-start(f32[8,2,64,256]{3,2,1,0:T(8,128)S(1)} %get-tuple-element.248), channel_id=1, source_target_pairs={{2,0},{3,1},{4,2},{5,3},{6,4},{7,5},{10,8},{11,9},{12,10},{13,11},... | collective-permute-start | bytes 3145736 | tf_op jit(solution)/shard_map/ppermute | solution.py:518
  345.0 36.8 %collective-permute-start.36 = (f32[8,2,64,256]{3,2,1,0:T(8,128)S(1)}, f32[8,2,64,256]{3,2,1,0:T(8,128)S(1)}, u32[]{:S(2)}, u32[]{:S(2)}) collective-permute-start(f32[8,2,64,256]{3,2,1,0:T(8,128)S(1)} %get-tuple-element.245), channel_id=1, source_target_pairs={{0,2},{1,3},{2,4},{3,5},{4,6},{5,7},{8,10},{9,11},{10,12},{11,13},... | collective-permute-start | bytes 3145736 | tf_op jit(solution)/shard_map/ppermute | solution.py:518
  350.5 37.3 %collective-permute-start.37 = (f32[8,2,64,256]{3,2,1,0:T(8,128)S(1)}, f32[8,2,64,256]{3,2,1,0:T(8,128)S(1)}, u32[]{:S(2)}, u32[]{:S(2)}) collective-permute-start(f32[8,2,64,256]{3,2,1,0:T(8,128)S(1)} %get-tuple-element.246), channel_id=1, source_target_pairs={{2,0},{3,1},{4,2},{5,3},{6,4},{7,5},{10,8},{11,9},{12,10},{13,11},... | collective-permute-start | bytes 3145736 | tf_op jit(solution)/shard_map/ppermute | solution.py:518
  367.4 36.9 %collective-permute-start.40 = (f32[8,2,64,256]{3,2,1,0:T(8,128)S(1)}, f32[8,2,64,256]{3,2,1,0:T(8,128)}, u32[]{:S(2)}, u32[]{:S(2)}) collective-permute-start(f32[8,2,64,256]{3,2,1,0:T(8,128)S(1)} %get-tuple-element.258), channel_id=1, source_target_pairs={{0,2},{1,3},{2,4},{3,5},{4,6},{5,7},{8,10},{9,11},{10,12},{11,13},... | collective-permute-start | bytes 3145736 | tf_op jit(solution)/shard_map/ppermute | solution.py:518
  373.3 37.1 %collective-permute-start.41 = (f32[8,2,64,256]{3,2,1,0:T(8,128)S(1)}, f32[8,2,64,256]{3,2,1,0:T(8,128)}, u32[]{:S(2)}, u32[]{:S(2)}) collective-permute-start(f32[8,2,64,256]{3,2,1,0:T(8,128)S(1)} %get-tuple-element.259), channel_id=1, source_target_pairs={{2,0},{3,1},{4,2},{5,3},{6,4},{7,5},{10,8},{11,9},{12,10},{13,11},... | collective-permute-start | bytes 3145736 | tf_op jit(solution)/shard_map/ppermute | solution.py:518
  (36 other events, 847.3 us)
